TPU v7x, 256 devices: a whole 4x4x8 slice. The times are simulated.
256 devices in a mesh: disp: 16 (over y, x_hi, core), col: 16 (over z, x_lo).
Axes of the slice: x: 4 (x_hi: 2, x_lo: 2; x = x_hi * 2 + x_lo), y: 4, z: 8, core: 2. Of those that a mesh axis runs over, the one named last changes fastest.
Arguments:
- left_feat: bfloat16 [320, 2, 4096], P('disp', None, 'col'), may hold values from -6 to 6
- right_feat: bfloat16 [320, 2, 4096], P('disp', None, 'col'), may hold values from -6 to 6
- conv1_w: bfloat16 [32, 40, 3, 3, 3], replicated, may hold values from -0.25 to 0.25
- conv2_w: bfloat16 [32, 32, 3, 3, 3], replicated, may hold values from -0.3125 to 0.3125
- conv3_w: bfloat16 [32, 32, 3, 3, 3], replicated, may hold values from -0.3125 to 0.3125
- head_w: float32 [32], replicated, may hold values from -120 to 120
Outputs:
- warped: bfloat16 [320, 2, 4096], P('disp', None, 'col')
- disparity: float32 [2, 4096], P(None, 'col')
All inputs are finite; a program needn't handle non-finite values.
Results may differ from a plain program's by a relative error of at most 0.015.
The roundings to bfloat16 on the way count: a program that leaves them out, or rounds other values in their place, can miss the bound.
Values may be sent and summed in bfloat16 or wider, within the bound.
A program may use at most 64 MiB of HBM per device.

v0:
```python
import jax
import jax.numpy as jnp
from jax import lax
from jax.sharding import PartitionSpec as P

G = 40
DG = 16
CG = 8


masked_value = -1e30


def with_halo(x, sides, width):
    for axis, dim in sides:
        peers, length = (lax.axis_size(axis), x.shape[dim])
        up = [(i, (i + 1) % peers) for i in range(peers - 1)]
        down = [(j, i) for i, j in up]
        last = lax.slice_in_dim(x, length - width, length, axis=dim)
        initial = lax.slice_in_dim(x, 0, width, axis=dim)
        before = lax.ppermute(last, axis, up)
        after = lax.ppermute(initial, axis, down)
        x = jnp.concatenate([before, x, after], axis=dim)
    return x


def passed_along(value, axis, steps):
    count = lax.axis_size(axis)
    initial, last = (max(0, -steps), min(count, count - steps))
    return lax.ppermute(value, axis, [(source, source + steps) for source in range(initial, last)])


def convolve(activity, kernel):
    padded = jnp.pad(activity, ((0, 0), (0, 0), (1, 1), (0, 0)))
    output = lax.conv_general_dilated(
        padded[None],
        kernel,
        (1, 1, 1),
        "VALID",
        dimension_numbers=("NCDHW", "OIDHW", "NCDHW"),
        preferred_element_type=jnp.float32,
    )
    return jnp.maximum(output[0], 0.0)


def layer_step(activity, kernel):
    widened = with_halo(activity, (("disp", 1), ("col", 3)), 1)
    return convolve(widened, kernel)


def accumulate(weighting, right_rows, start_base, strip_width):
    group_depth = weighting.shape[0]

    def add_term(offset, running):
        shifted = lax.dynamic_slice_in_dim(right_rows, start_base - offset, strip_width, 2)
        weight = lax.dynamic_index_in_dim(weighting, offset, 0, keepdims=False)
        return running + weight[None] * shifted.astype(jnp.float32)

    initial = jnp.zeros((right_rows.shape[0], right_rows.shape[1], strip_width), jnp.float32)
    return lax.fori_loop(0, group_depth, add_term, initial)


def shards(left_feat, right_feat, conv1_w, conv2_w, conv3_w, head_w):
    groups_disp = lax.axis_size("disp")
    slab_rows = left_feat.shape[1]
    strip_width = left_feat.shape[2]
    group_depth = DG
    disp_span = group_depth * groups_disp
    group_index = lax.axis_index("disp")
    strip_index = lax.axis_index("col")
    first_disp = group_index * group_depth
    left_full, right_full = (
        lax.all_gather(left_feat, "disp", axis=0, tiled=True),
        lax.all_gather(right_feat, "disp", axis=0, tiled=True),
    )
    tail_columns = passed_along(right_full, "col", 1)
    right_wide = jnp.concatenate([tail_columns, right_full], axis=2)
    start_base = disp_span - first_disp

    def correlate(offset):
        shifted = lax.dynamic_slice_in_dim(right_wide, start_base - offset, strip_width, 2)
        product = left_full.astype(jnp.float32) * shifted.astype(jnp.float32)
        return (jnp.sum(product.reshape(G, CG, slab_rows, strip_width), axis=1) / CG).astype(
            jnp.bfloat16
        )

    volume = jnp.moveaxis(lax.map(correlate, jnp.arange(group_depth, dtype=jnp.int32)), 0, 1)
    activity = layer_step(volume, conv1_w).astype(jnp.bfloat16)
    activity = layer_step(activity, conv2_w).astype(jnp.bfloat16)
    activity = layer_step(activity, conv3_w)
    scores = jnp.sum(head_w[:, None, None, None] * activity, axis=0)
    disp_global = first_disp + jnp.arange(group_depth, dtype=jnp.int32)
    column_global = strip_index * strip_width + jnp.arange(strip_width, dtype=jnp.int32)
    valid_mask = column_global[None, None, :] >= disp_global[:, None, None]
    scores = jnp.where(valid_mask, scores, masked_value)
    local_top = jnp.max(scores, axis=0)
    disp_values = disp_global.astype(jnp.float32)[:, None, None]
    top_score = lax.pmax(local_top, "disp")
    weighting = jnp.where(valid_mask, jnp.exp(scores - top_score[None]), 0.0)
    denominator, disp_sum = lax.psum(
        (jnp.sum(weighting, axis=0), jnp.sum(weighting * disp_values, axis=0)), "disp"
    )
    numerator = lax.psum_scatter(
        accumulate(weighting, right_wide, start_base, strip_width),
        "disp",
        scatter_dimension=0,
        tiled=True,
    )
    warped = (numerator / denominator[None]).astype(jnp.bfloat16)
    return (warped, disp_sum / denominator / disp_span)


def solution(mesh):
    return jax.shard_map(
        shards,
        mesh=mesh,
        in_specs=(P("disp", None, "col"), P("disp", None, "col"), P(), P(), P(), P()),
        out_specs=(P("disp", None, "col"), P(None, "col")),
        check_vma=False,
    )
```

profile of v0, /device:TPU:1, one launch (start us, length us, event | category | flops | bytes accessed | tf_op | source)
XLA Modules:
  0.0 503.7 jit_solution(17705847507461194090)
XLA Ops:
  7.2 27.4 %all_gather.7 = bf16[320,2,256]{2,1,0:T(2,128)(2,1)S(1)} all-gather(bf16[20,2,256]{2,1,0:T(2,128)(2,1)} %param.11), channel_id=1, replica_groups=mesh['disp'=16,'col'=16] {'disp'}, dimensions={0}, use_global_device_ids=true | all-gather | bytes 348160 | tf_op jit(solution)/shard_map/all_gather | solution.py:74
  34.6 2.2 collective-permute-start
  36.9 26.7 %all_gather.6 = bf16[320,2,256]{2,1,0:T(2,128)(2,1)S(1)} all-gather(bf16[20,2,256]{2,1,0:T(2,128)(2,1)} %param.10), channel_id=1, replica_groups=mesh['disp'=16,'col'=16] {'disp'}, dimensions={0}, use_global_device_ids=true | all-gather | bytes 348160 | tf_op jit(solution)/shard_map/all_gather | solution.py:73
  64.1 37.7 %while.24 = (s32[]{:T(128)}, bf16[16,40,2,256]{3,2,1,0:T(2,128)(2,1)S(1)}, bf16[320,2,256]{2,1,0:T(2,128)(2,1)S(1)}, s32[16]{0:T(128)S(1)}, s32[]{:T(128)}, /*in...) while((s32[]{:T(128)}, bf16[16,40,2,256]{3,2,1,0:T(2,128)(2,1)S(1)}, ...), condition=%wide.region_2.3_spmd, body=%wide.region_0.2_spmd.sunk | while | flops 675846 | bytes 2171051 | solution.py:87
  101.9 1.9 collective-permute-start.1
  103.8 2.4 collective-permute-start.2
  106.3 4.4 collective-permute-done.2
  110.7 1.1 pad_maximum_fusion
  112.5 1.6 collective-permute-start.3
  114.1 1.5 collective-permute-start.4
  115.5 11.5 %collective-permute-done.3 = bf16[40,18,2,1]{3,2,0,1:T(2,128)(2,1)S(1)} collective-permute-done((bf16[40,18,2,1]{3,2,0,1:T(2,128)(2,1)S(1)}, bf16[40,18,2,1]{3,2,0,1:T(2,128)(2,1)S(1)}, u32[]{:S(2)}, u32[]{:S(2)}) %collective-permute-start.3) | collective-permute-done | bytes 2912 | tf_op jit(solution)/shard_map/ppermute | solution.py:21
  127.1 6.5 %fusion.31 = bf16[40,18,4,1,258]{4,2,0,1,3:T(4,128)(2,1)S(1)} fusion(bf16[40,18,2,1]{3,2,0,1:T(2,128)(2,1)S(1)} %collective-permute-done.4, bf16[40,18,2,1]{3,2,0,1:T(2,128)(2,1)S(1)} %collective-permute-done.3, bf16[40,1,2,256]{3,2,0,1:T(2,128)(2,1)S(1)} %collective-permute-done.2, bf16[40,16,2,256]{3,2,0,1:T(2,128)(2,1)S(1)} %bitcast.83, ...), kind=kLoop, calls=%fused_computation.42 | loop fusion | flops 13374720 | bytes 2229120 | tf_op jit(solution)/shard_map/broadcast_in_dim | solution.py:36
  134.6 6.3 %reshape.109 = bf16[40,18,4,1,8,33]{5,4,2,0,1,3:T(8,128)(2,1)} reshape(bf16[40,18,4,1,264]{4,2,0,1,3:T(4,128)(2,1)S(1)} %pad.14) | data formatting | bytes 3041280 | tf_op jit(solution)/shard_map/conv_general_dilated | solution.py:35
  140.9 9.4 %copy.20 = bf16[40,18,4,1,8,33]{0,4,5,2,1,3:T(8,128)(2,1)} copy(bf16[40,18,4,1,8,33]{5,4,2,0,1,3:T(8,128)(2,1)} %reshape.109) | data formatting | bytes 3041280 | tf_op jit(solution)/shard_map/conv_general_dilated | solution.py:35
  150.2 1.0 slice.58
  151.3 13.6 %maximum_convert_fusion.1 = bf16[16,2,8,33,32]{4,2,3,1,0:T(8,128)(2,1)} fusion(pred[8,33]{0,1:T(8,128)(4,1)S(1)} %copy-done.7, bf16[32,40,3,3,3]{1,0,4,3,2:T(8,128)(2,1)S(1)} %copy-done, bf16[40,18,4,1,7,2]{0,4,5,2,1,3:T(8,128)(2,1)S(1)} %slice.58, bf16[40,18,4,1,8,33]{0,4,5,2,1,3:T(8,128)(2,1)} %copy.20), kind=kOutput, calls=%fused_computation.36 | convolution fusion | flops 589575168 | bytes 2211336 | tf_op jit(solution)/shard_map/conv_general_dilated | solution.py:35
  164.9 3.8 copy.21
  168.6 2.2 reshape.78
  170.9 1.1 slice_bitcast_fusion.2
  172.0 5.5 %collective-permute-start.5 = (bf16[32,1,2,256]{3,0,2,1:T(8,128)(2,1)S(1)}, bf16[32,1,2,256]{3,0,2,1:T(8,128)(2,1)S(1)}, u32[]{:S(2)}, u32[]{:S(2)}) collective-permute-start(bf16[32,1,2,256]{3,0,2,1:T(8,128)(2,1)S(1)} %get-tuple-element.185), channel_id=1, source_target_pairs={{0,16},{16,32},{32,48},{48,64},{64,80},{80,96},{96,112},{112,128},... | collective-permute-start | bytes 98312 | tf_op jit(solution)/shard_map/ppermute | solution.py:21
  177.5 1.9 collective-permute-start.6
  179.5 4.8 collective-permute-done.6
  184.5 3.5 collective-permute-start.7
  188.0 1.5 collective-permute-start.8
  189.6 2.1 collective-permute-done.7
  191.7 7.4 %collective-permute-done.8 = bf16[32,18,2,1]{3,0,2,1:T(8,128)(2,1)S(1)} collective-permute-done((bf16[32,18,2,1]{3,0,2,1:T(8,128)(2,1)S(1)}, bf16[32,18,2,1]{3,0,2,1:T(8,128)(2,1)S(1)}, u32[]{:S(2)}, u32[]{:S(2)}) %collective-permute-start.8) | collective-permute-done | bytes 2336 | tf_op jit(solution)/shard_map/ppermute | solution.py:22
  200.3 5.4 %reshape.81 = bf16[32,18,4,1,8,33]{5,4,0,2,1,3:T(8,128)(2,1)} reshape(bf16[32,18,4,1,264]{4,0,2,1,3:T(8,128)(2,1)S(1)} %pad.16) | data formatting | bytes 2433024 | tf_op jit(solution)/shard_map/conv_general_dilated | solution.py:35
  205.8 9.1 %copy.23 = bf16[32,18,4,1,8,33]{0,4,5,2,1,3:T(8,128)(2,1)} copy(bf16[32,18,4,1,8,33]{5,4,0,2,1,3:T(8,128)(2,1)} %reshape.81) | data formatting | bytes 2433024 | tf_op jit(solution)/shard_map/conv_general_dilated | solution.py:35
  214.8 1.0 slice.64
  215.9 9.1 %maximum_convert_fusion = bf16[16,2,8,33,32]{4,2,3,1,0:T(8,128)(2,1)} fusion(pred[8,33]{0,1:T(8,128)(4,1)S(1)} %copy-done.7, bf16[32,32,3,3,3]{1,0,4,3,2:T(8,128)(2,1)S(1)} %copy-done.4, bf16[32,18,4,1,7,2]{0,4,5,2,1,3:T(8,128)(2,1)S(1)} %slice.64, bf16[32,18,4,1,8,33]{0,4,5,2,1,3:T(8,128)(2,1)} %copy.23), kind=kOutput, calls=%fused_computation.35 | convolution fusion | flops 471822336 | bytes 1877256 | tf_op jit(solution)/shard_map/conv_general_dilated | solution.py:35
  225.0 3.8 copy.24
  228.8 2.2 reshape.85
  231.0 1.1 slice_bitcast_fusion.1
  232.1 1.9 collective-permute-start.10
  234.0 5.1 %collective-permute-start.9 = (bf16[32,1,2,256]{3,0,2,1:T(8,128)(2,1)S(1)}, bf16[32,1,2,256]{3,0,2,1:T(8,128)(2,1)S(1)}, u32[]{:S(2)}, u32[]{:S(2)}) collective-permute-start(bf16[32,1,2,256]{3,0,2,1:T(8,128)(2,1)S(1)} %get-tuple-element.183), channel_id=1, source_target_pairs={{0,16},{16,32},{32,48},{48,64},{64,80},{80,96},{96,112},{112,128},... | collective-permute-start | bytes 98312 | tf_op jit(solution)/shard_map/ppermute | solution.py:21
  240.4 4.6 collective-permute-start.11
  245.0 1.6 collective-permute-start.12
  246.6 2.8 collective-permute-done.11
  249.4 7.1 %collective-permute-done.12 = bf16[32,18,2,1]{3,0,2,1:T(8,128)(2,1)S(1)} collective-permute-done((bf16[32,18,2,1]{3,0,2,1:T(8,128)(2,1)S(1)}, bf16[32,18,2,1]{3,0,2,1:T(8,128)(2,1)S(1)}, u32[]{:S(2)}, u32[]{:S(2)}) %collective-permute-start.12) | collective-permute-done | bytes 2336 | tf_op jit(solution)/shard_map/ppermute | solution.py:22
  257.7 5.4 %reshape.88 = bf16[32,18,4,1,8,33]{5,4,0,2,1,3:T(8,128)(2,1)} reshape(bf16[32,18,4,1,264]{4,0,2,1,3:T(8,128)(2,1)S(1)} %pad.18) | data formatting | bytes 2433024 | tf_op jit(solution)/shard_map/conv_general_dilated | solution.py:35
  263.1 9.1 %copy.26 = bf16[32,18,4,1,8,33]{0,4,5,2,1,3:T(8,128)(2,1)} copy(bf16[32,18,4,1,8,33]{5,4,0,2,1,3:T(8,128)(2,1)} %reshape.88) | data formatting | bytes 2433024 | tf_op jit(solution)/shard_map/conv_general_dilated | solution.py:35
  272.2 1.0 slice.70
  273.3 9.5 %select_maximum_fusion = f32[16,2,8,33,32]{4,2,3,1,0:T(8,128)} fusion(pred[8,33]{0,1:T(8,128)(4,1)S(1)} %copy-done.7, bf16[32,32,3,3,3]{1,0,4,3,2:T(8,128)(2,1)S(1)} %copy-done.5, bf16[32,18,4,1,7,2]{0,4,5,2,1,3:T(8,128)(2,1)S(1)} %slice.70, bf16[32,18,4,1,8,33]{0,4,5,2,1,3:T(8,128)(2,1)} %copy.26), kind=kOutput, calls=%fused_computation.34 | convolution fusion | flops 471552000 | bytes 2417928 | tf_op jit(solution)/shard_map/conv_general_dilated | solution.py:35
  282.7 5.7 %copy.27 = f32[16,2,8,33,32]{3,2,4,1,0:T(8,128)} copy(f32[16,2,8,33,32]{4,2,3,1,0:T(8,128)} %select_maximum_fusion) | data formatting | bytes 2162688 | tf_op jit(solution)/shard_map/max | solution.py:43
  288.5 3.5 reshape.92
  292.2 34.3 %pmax.7 = f32[2,256]{1,0:T(2,128)S(1)} all-reduce(f32[2,256]{1,0:T(2,128)S(1)} %fusion.62), channel_id=1, replica_groups=mesh['disp'=16,'col'=16] {'disp'}, use_global_device_ids=true, to_apply=%region_5.6 | all-reduce | flops 512 | bytes 4096 | tf_op jit(solution)/shard_map/pmax | solution.py:98
  326.7 16.9 %while.25 = (s32[]{:T(128)}, f32[320,2,256]{2,1,0:T(2,128)S(1)}, f32[16,2,256]{2,1,0:T(2,128)S(1)}, s32[]{:T(128)}, bf16[320,2,512]{2,1,0:T(2,128)(2,1)S(1)}, /*index=5*/s32[]{:T(128)}, s32[]{:T(128)}, s32[]{:T(128)}) while((s32[]{:T(128)}, f32[320,2,256]{2,1,0:T(2,128)S(1)}, f32[16,2,256]{2,1,0:T(2,128)S(1)}, s32[]{:T(128)}, ...), condition=%wide.region_7.8_spmd.clone, body=%wide.region_6.7_spmd.clone.sunk | while | flops 655367 | bytes 1644693 | solution.py:60
  326.7 1.0 select_add_fusion.2
  327.8 1.0 select_add_fusion.2
  328.8 1.0 select_add_fusion.2
  329.9 1.0 select_add_fusion.2
  330.9 1.0 select_add_fusion.2
  332.0 1.0 select_add_fusion.2
  333.0 1.0 select_add_fusion.2
  334.1 1.0 select_add_fusion.2
  335.1 1.0 select_add_fusion.2
  336.2 1.0 select_add_fusion.2
  337.2 1.0 select_add_fusion.2
  338.3 1.0 select_add_fusion.2
  339.3 1.0 select_add_fusion.2
  340.4 1.0 select_add_fusion.2
  345.7 33.1 %all-reduce.4 = (f32[2,256]{1,0:T(2,128)S(1)}, f32[2,256]{1,0:T(2,128)S(1)}) all-reduce(f32[2,256]{1,0:T(2,128)S(1)} %get-tuple-element.149, f32[2,256]{1,0:T(2,128)S(1)} %get-tuple-element.148), channel_id=1, replica_groups=mesh['disp'=16,'col'=16] {'disp'}, use_global_device_ids=true, to_apply=%region_10.11 | all-reduce | flops 1024 | bytes 8192 | tf_op jit(solution)/shard_map/psum | solution.py:100
  379.4 116.0 %all-reduce.7.cloned.1.call-done = f32[320,2,256]{2,1,0:T(2,128)} async-done(((f32[320,2,256]{2,1,0:T(2,128)}), f32[320,2,256]{2,1,0:T(2,128)}) %all-reduce.7.cloned.1.call-update) | async-done | bytes 655376
  495.4 1.4 fusion.61
  (133 shorter events, 38.0 us)
Async XLA Ops:
  7.2 144.1 %copy-start = (bf16[32,40,3,3,3]{1,0,4,3,2:T(8,128)(2,1)S(1)}, bf16[32,40,3,3,3]{1,0,4,3,2:T(8,128)(2,1)}, u32[]{:S(2)}) copy-start(bf16[32,40,3,3,3]{1,0,4,3,2:T(8,128)(2,1)} %param.12) | copy-start | bytes 207364
  7.2 488.2 %all-reduce.7.cloned.1.call-start = ((), (), s32[]{:S(2)}) async-start(), calls=%async_computation | async-start | bytes 1310720
  34.6 28.9 %collective-permute-start = (bf16[320,2,256]{2,1,0:T(2,128)(2,1)S(1)}, bf16[320,2,256]{2,1,0:T(2,128)(2,1)S(1)}, u32[]{:S(2)}, u32[]{:S(2)}) collective-permute-start(bf16[320,2,256]{2,1,0:T(2,128)(2,1)S(1)} %all_gather.7), channel_id=1, source_target_pairs={{0,1},{1,2},{2,3},{3,4},{4,5},{5,6},{6,7},{7,8},{8,9},{9,10},{10,1... | collective-permute-start | bytes 983048 | tf_op jit(solution)/shard_map/ppermute | solution.py:30
  101.9 4.3 collective-permute-start.1
  103.8 6.8 %collective-permute-start.2 = (bf16[40,1,2,256]{3,2,0,1:T(2,128)(2,1)S(1)}, bf16[40,1,2,256]{3,2,0,1:T(2,128)(2,1)S(1)}, u32[]{:S(2)}, u32[]{:S(2)}) collective-permute-start(bf16[40,1,2,256]{3,2,0,1:T(2,128)(2,1)S(1)} %get-tuple-element.178), channel_id=1, source_target_pairs={{16,0},{32,16},{48,32},{64,48},{80,64},{96,80},{112,96},{128,112},... | collective-permute-start | bytes 122888 | tf_op jit(solution)/shard_map/ppermute | solution.py:22
  112.5 14.6 %collective-permute-start.3 = (bf16[40,18,2,1]{3,2,0,1:T(2,128)(2,1)S(1)}, bf16[40,18,2,1]{3,2,0,1:T(2,128)(2,1)S(1)}, u32[]{:S(2)}, u32[]{:S(2)}) collective-permute-start(bf16[40,18,2,1]{3,2,0,1:T(2,128)(2,1)S(1)} %get-tuple-element.175), channel_id=1, source_target_pairs={{0,1},{1,2},{2,3},{3,4},{4,5},{5,6},{6,7},{7,8},{8,9},{9,10},{10,1... | collective-permute-start | bytes 8648 | tf_op jit(solution)/shard_map/ppermute | solution.py:21
  114.1 13.0 %collective-permute-start.4 = (bf16[40,18,2,1]{3,2,0,1:T(2,128)(2,1)S(1)}, bf16[40,18,2,1]{3,2,0,1:T(2,128)(2,1)S(1)}, u32[]{:S(2)}, u32[]{:S(2)}) collective-permute-start(bf16[40,18,2,1]{3,2,0,1:T(2,128)(2,1)S(1)} %get-tuple-element.176), channel_id=1, source_target_pairs={{1,0},{2,1},{3,2},{4,3},{5,4},{6,5},{7,6},{8,7},{9,8},{10,9},{11,1... | collective-permute-start | bytes 8648 | tf_op jit(solution)/shard_map/ppermute | solution.py:22
  140.9 10.4 %copy-start.7 = (pred[8,33]{0,1:T(8,128)(4,1)S(1)}, pred[8,33]{0,1:T(8,128)(4,1)}, u32[]{:S(2)}) copy-start(pred[8,33]{0,1:T(8,128)(4,1)} %constant.93) | copy-start | bytes 796
  172.0 7.5 %collective-permute-start.5 = (bf16[32,1,2,256]{3,0,2,1:T(8,128)(2,1)S(1)}, bf16[32,1,2,256]{3,0,2,1:T(8,128)(2,1)S(1)}, u32[]{:S(2)}, u32[]{:S(2)}) collective-permute-start(bf16[32,1,2,256]{3,0,2,1:T(8,128)(2,1)S(1)} %get-tuple-element.185), channel_id=1, source_target_pairs={{0,16},{16,32},{32,48},{48,64},{64,80},{80,96},{96,112},{112,128},... | collective-permute-start | bytes 98312 | tf_op jit(solution)/shard_map/ppermute | solution.py:21
  177.5 6.7 %collective-permute-start.6 = (bf16[32,1,2,256]{3,0,2,1:T(8,128)(2,1)S(1)}, bf16[32,1,2,256]{3,0,2,1:T(8,128)(2,1)S(1)}, u32[]{:S(2)}, u32[]{:S(2)}) collective-permute-start(bf16[32,1,2,256]{3,0,2,1:T(8,128)(2,1)S(1)} %get-tuple-element.186), channel_id=1, source_target_pairs={{16,0},{32,16},{48,32},{64,48},{80,64},{96,80},{112,96},{128,112},... | collective-permute-start | bytes 98312 | tf_op jit(solution)/shard_map/ppermute | solution.py:22
  184.5 7.2 %collective-permute-start.7 = (bf16[32,18,2,1]{3,0,2,1:T(8,128)(2,1)S(1)}, bf16[32,18,2,1]{3,0,2,1:T(8,128)(2,1)S(1)}, u32[]{:S(2)}, u32[]{:S(2)}) collective-permute-start(bf16[32,18,2,1]{3,0,2,1:T(8,128)(2,1)S(1)} %get-tuple-element.181), channel_id=1, source_target_pairs={{0,1},{1,2},{2,3},{3,4},{4,5},{5,6},{6,7},{7,8},{8,9},{9,10},{10,1... | collective-permute-start | bytes 6920 | tf_op jit(solution)/shard_map/ppermute | solution.py:21
  188.0 11.0 %collective-permute-start.8 = (bf16[32,18,2,1]{3,0,2,1:T(8,128)(2,1)S(1)}, bf16[32,18,2,1]{3,0,2,1:T(8,128)(2,1)S(1)}, u32[]{:S(2)}, u32[]{:S(2)}) collective-permute-start(bf16[32,18,2,1]{3,0,2,1:T(8,128)(2,1)S(1)} %get-tuple-element.182), channel_id=1, source_target_pairs={{1,0},{2,1},{3,2},{4,3},{5,4},{6,5},{7,6},{8,7},{9,8},{10,9},{11,1... | collective-permute-start | bytes 6920 | tf_op jit(solution)/shard_map/ppermute | solution.py:22
  205.8 10.1 %copy-start.4 = (bf16[32,32,3,3,3]{1,0,4,3,2:T(8,128)(2,1)S(1)}, bf16[32,32,3,3,3]{1,0,4,3,2:T(8,128)(2,1)}, u32[]{:S(2)}) copy-start(bf16[32,32,3,3,3]{1,0,4,3,2:T(8,128)(2,1)} %param.13) | copy-start | bytes 165892
  232.1 7.2 %collective-permute-start.10 = (bf16[32,1,2,256]{3,0,2,1:T(8,128)(2,1)S(1)}, bf16[32,1,2,256]{3,0,2,1:T(8,128)(2,1)S(1)}, u32[]{:S(2)}, u32[]{:S(2)}) collective-permute-start(bf16[32,1,2,256]{3,0,2,1:T(8,128)(2,1)S(1)} %get-tuple-element.184), channel_id=1, source_target_pairs={{16,0},{32,16},{48,32},{64,48},{80,64},{96,80},{112,96},{128,112},... | collective-permute-start | bytes 98312 | tf_op jit(solution)/shard_map/ppermute | solution.py:22
  234.0 6.2 %collective-permute-start.9 = (bf16[32,1,2,256]{3,0,2,1:T(8,128)(2,1)S(1)}, bf16[32,1,2,256]{3,0,2,1:T(8,128)(2,1)S(1)}, u32[]{:S(2)}, u32[]{:S(2)}) collective-permute-start(bf16[32,1,2,256]{3,0,2,1:T(8,128)(2,1)S(1)} %get-tuple-element.183), channel_id=1, source_target_pairs={{0,16},{16,32},{32,48},{48,64},{64,80},{80,96},{96,112},{112,128},... | collective-permute-start | bytes 98312 | tf_op jit(solution)/shard_map/ppermute | solution.py:21
  240.4 8.9 %collective-permute-start.11 = (bf16[32,18,2,1]{3,0,2,1:T(8,128)(2,1)S(1)}, bf16[32,18,2,1]{3,0,2,1:T(8,128)(2,1)S(1)}, u32[]{:S(2)}, u32[]{:S(2)}) collective-permute-start(bf16[32,18,2,1]{3,0,2,1:T(8,128)(2,1)S(1)} %get-tuple-element.179), channel_id=1, source_target_pairs={{0,1},{1,2},{2,3},{3,4},{4,5},{5,6},{6,7},{7,8},{8,9},{9,10},{10,1... | collective-permute-start | bytes 6920 | tf_op jit(solution)/shard_map/ppermute | solution.py:21
  245.0 11.4 %collective-permute-start.12 = (bf16[32,18,2,1]{3,0,2,1:T(8,128)(2,1)S(1)}, bf16[32,18,2,1]{3,0,2,1:T(8,128)(2,1)S(1)}, u32[]{:S(2)}, u32[]{:S(2)}) collective-permute-start(bf16[32,18,2,1]{3,0,2,1:T(8,128)(2,1)S(1)} %get-tuple-element.180), channel_id=1, source_target_pairs={{1,0},{2,1},{3,2},{4,3},{5,4},{6,5},{7,6},{8,7},{9,8},{10,9},{11,1... | collective-permute-start | bytes 6920 | tf_op jit(solution)/shard_map/ppermute | solution.py:22
  263.1 10.1 %copy-start.5 = (bf16[32,32,3,3,3]{1,0,4,3,2:T(8,128)(2,1)S(1)}, bf16[32,32,3,3,3]{1,0,4,3,2:T(8,128)(2,1)}, u32[]{:S(2)}) copy-start(bf16[32,32,3,3,3]{1,0,4,3,2:T(8,128)(2,1)} %param.14) | copy-start | bytes 165892
  288.5 3.5 copy-start.3
  326.6 170.2 %copy-start.1 = (bf16[32,40,3,3,3]{1,0,4,3,2:T(8,128)(2,1)S(1)}, bf16[32,40,3,3,3]{1,0,4,3,2:T(8,128)(2,1)}, u32[]{:S(2)}) copy-start(bf16[32,40,3,3,3]{1,0,4,3,2:T(8,128)(2,1)} %param.12) | copy-start | bytes 207364
  326.6 17.8 %copy-start.6 = (u32[256]{0:T(256)S(1)}, u32[256]{0:T(256)}, u32[]{:S(2)}) copy-start(u32[256]{0:T(256)} %constant.98) | copy-start | bytes 3076
  343.5 0.9 copy-start.2
Sparse Core Ops, SparseCore 0:
  344.5 150.8 all-reduce.6
where the time goes:
time: 505 us; the launch traced here: 504 us
  waiting for transfers between devices  157 us (31%)
  blocking collectives  122 us (24%)
  local copies, waits for them, and re-layouts  85.7 us (17%)
  other arithmetic  45.8 us (9%)
  starting transfers between devices  35.3 us (7%)
  matrix products  32.1 us (6%)
  between operations  15.1 us (3%)
  loops' own time  11.1 us (2%)
    unnamed x2, waiting for transfers between devices  116 us
    conv_general_dilated x9, local copies, waits for them, and re-layouts, convolve(): lax.conv_general_dilated(padded[None], kernel, (1, 1, 1), 'VALID', dimens...  47.8 us
    pmax x1, blocking collectives, shards(): top_score = lax.pmax(local_top, 'disp')  34.3 us
    psum x1, blocking collectives, shards(): lax.psum((jnp.sum(weighting, axis=0), jnp.sum(weighting * disp_values, ax...  33.1 us
    conv_general_dilated x3, matrix products, convolve(): lax.conv_general_dilated(padded[None], kernel, (1, 1, 1), 'VALID', dimens...  32.1 us
    all_gather x1, blocking collectives, shards(): lax.all_gather(right_feat, 'disp', axis=0, tiled=True)  27.4 us
    all_gather x1, blocking collectives, shards(): lax.all_gather(left_feat, 'disp', axis=0, tiled=True)  26.7 us
    ppermute x6, waiting for transfers between devices, with_halo(): after = lax.ppermute(initial, axis, down)  23.7 us
  transfers between devices with their start and end apart: 14, of which 9 were waited for; matrix products, arithmetic and copies ran while one was open for 0% of the time, Pallas kernels for 0%

commit v1 on v0

v1 whole, which is shorter than its diff:
```python
import jax
import jax.numpy as jnp
from jax import lax
from jax.experimental import pallas as pl
from jax.experimental.pallas import tpu as pltpu
from jax.sharding import PartitionSpec as P

N = 16
LANES = 128
DISP = 256
CH_ROWS = 40
WIDE_ROWS = 48
COLS0, COLS1, COLS2, COLS3 = 22, 20, 18, 16
F = 32
MASKED = -1e30
MESH = pl.DeviceIdType.MESH
NT = (((1,), (1,)), ((), ()))


def first_block(i):
    return lax.div(i + 7, 8) - 1


def places(block):
    for low, high, first in ((0, 0, -1), (1, 8, 0), (9, 15, 1)):
        slot = block - first
        if 0 <= slot < 4:
            yield slot, max(low, 7) if slot == 3 and high == 8 else low, high


def gather_kernel(own, wide, near, send_sem, recv_sem):
    i, j = lax.axis_index("disp"), lax.axis_index("col")
    base = first_block(i)

    def slot_filled(q):
        block = 2 * (j - 1) + base + q
        filled = (block >= 0) & (block < 2 * N)
        if q == 3:
            filled = filled & ((lax.rem(i, 8) == 0) | (lax.rem(i, 8) == 7))
        return filled

    slots = [wide.at[0], wide.at[1], near.at[0], near.at[1]]
    for q in range(4):

        @pl.when(jnp.logical_not(slot_filled(q)))
        def _(q=q):
            slots[q][...] = jnp.zeros(slots[q].shape, jnp.bfloat16)

    barrier = pltpu.get_barrier_semaphore()

    def greet(di, dj):
        pl.semaphore_signal(barrier, inc=1, device_id=(di, dj), device_id_type=MESH)

    def greet_strip(dj):
        @pl.loop(0, N)
        def _(step):
            greet(lax.rem(i + step, N), dj)

    @pl.loop(1, N)
    def _(step):
        greet(lax.rem(i + step, N), j)

    pl.when(j >= 1)(lambda: greet_strip(j - 1))
    pl.when((i == 0) & (j >= 2))(lambda: greet_strip(j - 2))
    pl.when((i == N - 1) & (j <= N - 2))(lambda: greet_strip(j + 1))
    targets = N - 1 + N * (j <= N - 2) + (j <= N - 3) + (j >= 1)
    pl.semaphore_wait(barrier, targets)

    def copy(go, src, dst, slot, di, dj, sem):
        rdma = pltpu.make_async_remote_copy(
            src_ref=src,
            dst_ref=dst,
            send_sem=send_sem.at[sem],
            recv_sem=recv_sem.at[slot],
            device_id=(di, dj),
            device_id_type=MESH,
        )
        rdma.start() if go else rdma.wait_send()

    def landing(half, slot):
        if slot < 2:
            return own.at[half, pl.ds(0, WIDE_ROWS)], wide.at[slot, i]
        return own.at[half], near.at[slot - 2, i]

    def push(go, di, dj, half, block, sem):
        for slot, low, high in places(block):

            @pl.when((di >= low) & (di <= high))
            def _(slot=slot):
                copy(go, *landing(half, slot), slot, di, dj, sem)

    def exchange(go):
        @pl.loop(0, N)
        def _(step):
            di = lax.rem(i + step, N)

            @pl.when(step > 0)
            def _():
                for half in range(2):
                    push(go, di, j, half, 2 + half, half * N + step)

            @pl.when(j <= N - 2)
            def _():
                for half in range(2):
                    push(go, di, j + 1, half, half, (2 + half) * N + step)

            @pl.when((di == 0) & (j <= N - 3))
            def _():
                copy(go, *landing(1, 0), 0, di, j + 2, 0)

            @pl.when((di == N - 1) & (j >= 1))
            def _():
                copy(go, *landing(0, 3), 3, di, j - 1, N)

    exchange(True)

    for half in range(2):
        for slot, low, high in places(2 + half):

            @pl.when((i >= low) & (i <= high))
            def _(half=half, slot=slot):
                pltpu.make_async_copy(*landing(half, slot), recv_sem.at[slot]).start()

    for q in range(4):

        @pl.when(slot_filled(q))
        def _(q=q):
            pltpu.make_async_copy(slots[q], slots[q], recv_sem.at[q]).wait()

    exchange(False)


def gather(own):
    return pl.pallas_call(
        gather_kernel,
        out_shape=(
            jax.ShapeDtypeStruct((2, N, WIDE_ROWS, LANES), jnp.bfloat16),
            jax.ShapeDtypeStruct((2, N, 2 * CH_ROWS, LANES), jnp.bfloat16),
        ),
        in_specs=[pl.BlockSpec(memory_space=pltpu.VMEM)],
        out_specs=(pl.BlockSpec(memory_space=pltpu.VMEM),) * 2,
        scratch_shapes=[
            pltpu.SemaphoreType.DMA((4 * N,)),
            pltpu.SemaphoreType.DMA((4,)),
        ],
        compiler_params=pltpu.CompilerParams(
            collective_id=0, has_side_effects=True, vmem_limit_bytes=32 * 2**20
        ),
        name="gather_features",
    )(own)


def dot(a, b, dims=(((1,), (0,)), ((), ()))):
    return lax.dot_general(a, b, dims, preferred_element_type=jnp.float32)


def iota(shape, dim):
    return lax.broadcasted_iota(jnp.int32, shape, dim)


def one_hot(mask):
    return jnp.where(mask, 1.0, 0.0).astype(jnp.bfloat16)


def spread_first(weights, out):
    rows, lane = iota((CH_ROWS, LANES), 0), iota((CH_ROWS, LANES), 1)
    r = lane % 16
    flat = weights[...].reshape(27 * F, CH_ROWS)
    parts = [
        dot(flat, one_hot((rows == lane // 16 * 5 + r // 2) & (r < 10) & (r % 2 == h))) for h in range(2)
    ]
    parts = [part.reshape(3, 3, 3, F, LANES) for part in parts]
    for a in range(3):
        for to in range(2):
            for ho in range(2):
                row = ((a * 2 + to) * 2 + ho) * F
                for ti in range(4):
                    e = ti - to
                    if 0 <= e < 3:
                        block = parts[0][a, 1 - ho, e] + parts[1][a, 2 - ho, e]
                    else:
                        block = jnp.zeros((F, LANES), jnp.float32)
                    out[row : row + F, ti * LANES : (ti + 1) * LANES] = block.astype(jnp.bfloat16)


def spread_later(weights, out):
    rows, lane = iota((F, LANES), 0), iota((F, LANES), 1)
    flat = weights[...].reshape(27 * F, F)
    parts = [dot(flat, one_hot(rows == lane - k * F)).reshape(3, 3, 3, F, LANES) for k in range(4)]
    for a in range(3):
        for to in range(2):
            for ho in range(2):
                row = ((a * 2 + to) * 2 + ho) * F
                for pair in range(2):
                    block = jnp.zeros((F, LANES), jnp.float32)
                    for k in range(4):
                        e, h = pair * 2 + k // 2 - to, k % 2
                        if 0 <= e < 3:
                            block = block + parts[k][a, 1 + h - ho, e]
                    out[row : row + F, pair * LANES : (pair + 1) * LANES] = block.astype(jnp.bfloat16)


def filter_pair(kernel, x):
    taps = dot(kernel, x)
    rows = 2 * 2 * F
    lane = iota((rows, DISP), 1)
    before = jnp.where(lane == DISP - 1, 0.0, pltpu.roll(taps[:rows], DISP - 1, 1))
    after = jnp.where(lane == 0, 0.0, pltpu.roll(taps[2 * rows :], 1, 1))
    return jnp.maximum(taps[rows : 2 * rows] + before + after, 0.0)


def filter_kernel(wide, near, w1, w2, w3, head, out, k1, k2, k3, right, x0, x1, x2, scores):
    i, j = lax.axis_index("disp"), lax.axis_index("col")
    spread_first(w1, k1)
    spread_later(w2, k2)
    spread_later(w3, k3)

    start = 16 * i - 2 - LANES * first_block(i)
    lane = iota((80, LANES), 1)
    r, lane80 = iota((16, 80), 0), iota((16, 80), 1)
    group_mask = jnp.where((lane80 // 16 == r // 2) & (lane80 % 2 == r % 2), 0.125, 0.0)
    pick = one_hot(iota((32, 2 * LANES), 1) == start - 1 + iota((32, 2 * LANES), 0))
    for s in range(8):
        pair = pl.ds(2 * s, 2)
        blocks = [ref[q, pair].astype(jnp.float32) for ref in (wide, near) for q in range(2)]
        turned = [
            pltpu.roll(block[:, :CH_ROWS].reshape(80, LANES), LANES - start, 1) for block in blocks
        ]
        for m in range(3):
            moved = jnp.where(lane < LANES - start, turned[m], turned[m + 1])
            right[s, :, m * LANES : (m + 1) * LANES] = moved.astype(jnp.bfloat16)
        left = [block[:, CH_ROWS:].reshape(80, LANES).astype(jnp.bfloat16) for block in blocks[2:]]
        picked = dot(pick[:, :LANES], left[0], NT) + dot(pick[:, LANES:], left[1], NT)
        spread = picked[:COLS0].reshape(COLS0, 1, 80) * group_mask[None]
        spread = spread.reshape(COLS0 * 16, 80).astype(jnp.bfloat16)
        products = dot(spread, right[s])
        for k in range(COLS0):
            strip = products[k * 16 : (k + 1) * 16]
            if k:
                strip = pltpu.roll(strip, 3 * LANES - k, 1)
            x0[k * LANES + s * 16 : k * LANES + s * 16 + 16] = strip[:, :DISP].astype(jnp.bfloat16)

    leftmost, rightmost = (i == 0) & (j == 0), (i == N - 1) & (j == N - 1)
    to = iota((LANES, DISP), 0) // 64
    for p in range(COLS1 // 2):
        y = filter_pair(k1[...], x0[p * 256 : p * 256 + 512])
        if p == 0:
            y = jnp.where(leftmost, 0.0, y)
        if p == COLS1 // 2 - 1:
            y = jnp.where(rightmost, 0.0, y)
        x1[p * LANES : (p + 1) * LANES] = y.astype(jnp.bfloat16)
    for p in range(COLS2 // 2):
        y = filter_pair(k2[...], x1[p * LANES : p * LANES + 256])
        if p == 0:
            y = jnp.where(leftmost & (to == 0), 0.0, y)
        if p == COLS2 // 2 - 1:
            y = jnp.where(rightmost & (to == 1), 0.0, y)
        x2[p * LANES : (p + 1) * LANES] = y.astype(jnp.bfloat16)
    for p in range(COLS3 // 2):
        y = filter_pair(k3[...], x2[p * LANES : p * LANES + 256])
        y = jnp.sum((y * head[...]).reshape(4, F, DISP), axis=1)
        for t in range(2):
            for h in range(2):
                row = h * 16 + 2 * p + t
                scores[row : row + 1] = y[2 * t + h : 2 * t + h + 1]

    disp = DISP - 1 - iota((32, DISP), 1)
    column = (N * j + i) * 16 + iota((32, DISP), 0) % 16
    valid = column >= disp
    score = jnp.where(valid, scores[...], MASKED)
    top = jnp.max(score, axis=1, keepdims=True)
    weighting = jnp.where(valid, jnp.exp(score - top), 0.0)
    denominator = jnp.sum(weighting, axis=1, keepdims=True)
    disparity = jnp.sum(weighting * disp.astype(jnp.float32), axis=1, keepdims=True) / denominator / DISP
    padded = jnp.concatenate([weighting, jnp.zeros((32, LANES), jnp.float32)], axis=1)
    band = jnp.concatenate(
        [pltpu.roll(padded[h * 16 : h * 16 + 16], 3, 1, stride=1, stride_axis=0) for h in range(2)], axis=0
    )
    high = band.astype(jnp.bfloat16)
    low = (band - high.astype(jnp.float32)).astype(jnp.bfloat16)
    band = jnp.concatenate([high, low], axis=0)
    out_lane = iota((16, LANES), 1)
    disp_high = disparity.astype(jnp.bfloat16).astype(jnp.float32)
    disp_low = disparity - disp_high
    tail = jnp.zeros((16, LANES), jnp.float32)
    for n, column_of in enumerate((disp_high[:16], disp_high[16:], disp_low[:16], disp_low[16:])):
        tail = jnp.where(out_lane == 80 + n, column_of, tail)
    even = iota((16, 80), 1) % 2 == 0
    for s in range(8):
        summed = dot(band, right[s], NT)
        warped = (summed[:32] + summed[32:]) / denominator
        picked = jnp.where(even, warped[:16], warped[16:])
        picked = jnp.concatenate([picked, jnp.zeros((16, LANES - 80), jnp.float32)], axis=1)
        out[s] = jnp.where(out_lane < 80, picked, tail).astype(jnp.bfloat16)


def filtered(wide, near, w1, w2, w3, head):
    vmem = pl.BlockSpec(memory_space=pltpu.VMEM)
    return pl.pallas_call(
        filter_kernel,
        out_shape=jax.ShapeDtypeStruct((8, 16, LANES), jnp.bfloat16),
        in_specs=[vmem] * 6,
        out_specs=vmem,
        scratch_shapes=[
            pltpu.VMEM((384, 512), jnp.bfloat16),
            pltpu.VMEM((384, 256), jnp.bfloat16),
            pltpu.VMEM((384, 256), jnp.bfloat16),
            pltpu.VMEM((8, 80, 384), jnp.bfloat16),
            pltpu.VMEM((COLS0 * 128, DISP), jnp.bfloat16),
            pltpu.VMEM((COLS1 * 64, DISP), jnp.bfloat16),
            pltpu.VMEM((COLS2 * 64, DISP), jnp.bfloat16),
            pltpu.VMEM((32, DISP), jnp.float32),
        ],
        compiler_params=pltpu.CompilerParams(vmem_limit_bytes=48 * 2**20),
        name="filter_columns",
    )(wide, near, w1, w2, w3, head)


def scatter_kernel(parts, warped, disparity, held, send_sem, recv_sem):
    i, j = lax.axis_index("disp"), lax.axis_index("col")
    barrier = pltpu.get_barrier_semaphore()

    @pl.loop(1, N)
    def _(step):
        pl.semaphore_signal(barrier, inc=1, device_id=(lax.rem(i + step, N), j), device_id_type=MESH)

    pl.semaphore_wait(barrier, N - 1)

    def push(step, go):
        di = lax.rem(i + step, N)
        rdma = pltpu.make_async_remote_copy(
            src_ref=parts.at[lax.div(di, 2)],
            dst_ref=held.at[i],
            send_sem=send_sem.at[step],
            recv_sem=recv_sem,
            device_id=(di, j),
            device_id_type=MESH,
        )
        rdma.start() if go else rdma.wait_send()

    pl.loop(1, N)(lambda step: push(step, True))
    pltpu.make_async_copy(parts.at[lax.div(i, 2)], held.at[i], recv_sem).start()
    pltpu.make_async_copy(held, held, recv_sem).wait()
    pl.loop(1, N)(lambda step: push(step, False))
    rows, lane = iota((48, LANES), 0), iota((48, LANES), 1)
    mine = lane == lax.rem(i, 2) * CH_ROWS + rows
    tail = (lane == 40 + rows) | (lane == 42 + rows)
    pick = one_hot((mine & (rows < CH_ROWS)) | (tail & (rows >= CH_ROWS) & (rows < CH_ROWS + 2)))
    result = dot(pick, held[...].reshape(256, LANES), NT)
    warped[...] = result[:CH_ROWS].astype(jnp.bfloat16)
    disparity[...] = result[CH_ROWS : CH_ROWS + 2]


def scattered(parts):
    vmem = pl.BlockSpec(memory_space=pltpu.VMEM)
    return pl.pallas_call(
        scatter_kernel,
        out_shape=(
            jax.ShapeDtypeStruct((CH_ROWS, 256), jnp.bfloat16),
            jax.ShapeDtypeStruct((2, 256), jnp.float32),
        ),
        in_specs=[vmem],
        out_specs=(vmem, vmem),
        scratch_shapes=[
            pltpu.VMEM((N, 16, LANES), jnp.bfloat16),
            pltpu.SemaphoreType.DMA((N,)),
            pltpu.SemaphoreType.DMA,
        ],
        compiler_params=pltpu.CompilerParams(collective_id=1, has_side_effects=True),
        name="scatter_results",
    )(parts)


def shards(left_feat, right_feat, conv1_w, conv2_w, conv3_w, head_w):
    own = jnp.concatenate([right_feat.reshape(CH_ROWS, 2, LANES), left_feat.reshape(CH_ROWS, 2, LANES)])
    own = jnp.transpose(own, (1, 0, 2))
    w1, w2, w3 = (jnp.transpose(w, (2, 3, 4, 0, 1)) for w in (conv1_w, conv2_w, conv3_w))
    head = jnp.tile(head_w, 4).reshape(128, 1)
    wide, near = gather(own)
    parts = filtered(wide, near, w1, w2, w3, head)
    warped, disparity = scattered(parts)
    return warped.reshape(20, 2, 256), disparity


def solution(mesh):
    return jax.shard_map(
        shards,
        mesh=mesh,
        in_specs=(P("disp", None, "col"), P("disp", None, "col"), P(), P(), P(), P()),
        out_specs=(P("disp", None, "col"), P(None, "col")),
        check_vma=False,
    )
```

time: 505 us -> 42.4 us (0.08)
  the two profiles are of different devices: /device:TPU:1 before, /device:TPU:129 now
where the time goes in v1:
time: 42.4 us; the launch traced here: 42.1 us
  Pallas kernels  34.7 us (82%)
  local copies, waits for them, and re-layouts  6.7 us (16%)
  between operations  0.73 us (2%)
    pallas_call x1, Pallas kernels, gather(): pl.pallas_call(gather_kernel, out_shape=(jax.ShapeDtypeStruct((2, N, WIDE...  19.4 us
    pallas_call x1, Pallas kernels, scattered(): pl.pallas_call(scatter_kernel, out_shape=(jax.ShapeDtypeStruct((CH_ROWS,...  9.83 us
    pallas_call x1, Pallas kernels, filtered(): pl.pallas_call(filter_kernel, out_shape=jax.ShapeDtypeStruct((8, 16, LANE...  5.39 us
    unnamed x13, local copies, waits for them, and re-layouts  3.69 us
    reshape x1, local copies, waits for them, and re-layouts, shards(): return (warped.reshape(20, 2, 256), disparity)  1.35 us

profile of v1, /device:TPU:129, one launch (start us, length us, event | category | flops | bytes accessed | tf_op | source)
XLA Modules:
  0.0 42.1 jit_solution(11238296993009770650)
XLA Ops:
  0.6 0.0 copy-start
  0.6 0.8 %reshape.15 = bf16[40,2,128]{2,1,0:T(2,128)(2,1)S(1)} reshape(bf16[20,2,256]{2,1,0:T(2,128)(2,1)} %param.6) | data formatting | bytes 40960 | tf_op jit(solution)/shard_map/reshape | solution.py:375
  1.4 0.7 %reshape.14 = bf16[40,2,128]{2,1,0:T(2,128)(2,1)S(1)} reshape(bf16[20,2,256]{2,1,0:T(2,128)(2,1)} %param.7) | data formatting | bytes 40960 | tf_op jit(solution)/shard_map/reshape | solution.py:375
  2.2 19.4 %gather_features.1 = (bf16[2,16,48,128]{3,2,1,0:T(8,128)(2,1)S(1)}, bf16[2,16,80,128]{3,2,1,0:T(8,128)(2,1)S(1)}) custom-call(bf16[2,80,128]{2,1,0:T(8,128)(2,1)S(1)} %maximum_bitcast_fusion.own), custom_call_target="tpu_custom_call" | custom-call | tf_op jit(solution)/shard_map/gather_features/pallas_call | solution.py:134
  21.7 0.0 copy-start.5
  21.7 0.6 %copy-done.5 = f32[32]{0:T(128)S(1)} copy-done((f32[32]{0:T(128)S(1)}, f32[32]{0:T(128)}, u32[]{:S(2)}) %copy-start.5) | copy-done | bytes 152
  22.3 0.1 reshape_tile.4.head
  22.4 0.0 copy-done
  22.5 0.0 copy-start.1
  22.5 0.9 %copy-done.1 = bf16[32,32,3,3,3]{1,0,4,3,2:T(8,128)(2,1)S(1)} copy-done((bf16[32,32,3,3,3]{1,0,4,3,2:T(8,128)(2,1)S(1)}, bf16[32,32,3,3,3]{1,0,4,3,2:T(8,128)(2,1)}, u32[]{:S(2)}) %copy-start.1) | copy-done | bytes 55320
  23.4 0.0 copy-start.2
  23.4 0.9 %copy-done.2 = bf16[32,32,3,3,3]{1,0,4,3,2:T(8,128)(2,1)S(1)} copy-done((bf16[32,32,3,3,3]{1,0,4,3,2:T(8,128)(2,1)S(1)}, bf16[32,32,3,3,3]{1,0,4,3,2:T(8,128)(2,1)}, u32[]{:S(2)}) %copy-start.2) | copy-done | bytes 55320
  24.3 5.4 %filter_columns.1.parts = bf16[8,16,128]{2,1,0:T(8,128)(2,1)S(1)} custom-call(bf16[2,16,48,128]{3,2,1,0:T(8,128)(2,1)S(1)} %get-tuple-element.6.wide, bf16[2,16,80,128]{3,2,1,0:T(8,128)(2,1)S(1)} %get-tuple-element.7.near, bf16[3,3,3,32,40]{4,3,2,1,0:T(8,128)(2,1)S(1)} %bitcast.5, bf16[3,3,3,32,32]{4,3,2,1,0:T(8,128)(2,1)S(1)} %bitcast.6, ...), custom_call_target="tpu_custom_call" | custom-call | tf_op jit(solution)/shard_map/filter_columns/pallas_call | solution.py:299
  29.7 0.0 copy-start.3
  29.7 0.6 %copy-done.3 = bf16[8,16,128]{2,1,0:T(8,128)(2,1)} copy-done((bf16[8,16,128]{2,1,0:T(8,128)(2,1)}, bf16[8,16,128]{2,1,0:T(8,128)(2,1)S(1)}, u32[]{:S(2)}) %copy-start.3) | copy-done | bytes 32792
  30.3 9.8 %scatter_results.1 = (bf16[40,256]{1,0:T(8,128)(2,1)}, f32[2,256]{1,0:T(2,128)}) custom-call(bf16[8,16,128]{2,1,0:T(8,128)(2,1)} %copy-done.3), custom_call_target="tpu_custom_call" | custom-call | tf_op jit(solution)/shard_map/scatter_results/pallas_call | solution.py:356
  40.2 0.0 copy-start.4
  40.2 1.3 %reshape.16 = bf16[20,2,256]{2,1,0:T(2,128)(2,1)} reshape(bf16[40,256]{1,0:T(8,128)(2,1)} %get-tuple-element.8) | data formatting | bytes 40960 | tf_op jit(solution)/shard_map/reshape | solution.py:382
  41.5 0.0 copy-done.4
  41.5 0.6 %copy.13 = f32[2,256]{1,0:T(2,128)} copy(f32[2,256]{1,0:T(2,128)S(1)} %copy-done.4) | data formatting | bytes 4096
  (4 shorter events, 0.0 us)
Async XLA Ops:
  0.6 21.8 %copy-start = (bf16[32,40,3,3,3]{1,0,4,3,2:T(8,128)(2,1)S(1)}, bf16[32,40,3,3,3]{1,0,4,3,2:T(8,128)(2,1)}, u32[]{:S(2)}) copy-start(bf16[32,40,3,3,3]{1,0,4,3,2:T(8,128)(2,1)} %param.8) | copy-start | bytes 207364
  21.7 0.7 %copy-start.5 = (f32[32]{0:T(128)S(1)}, f32[32]{0:T(128)}, u32[]{:S(2)}) copy-start(f32[32]{0:T(128)} %param.11) | copy-start | bytes 388
  22.5 0.9 %copy-start.1 = (bf16[32,32,3,3,3]{1,0,4,3,2:T(8,128)(2,1)S(1)}, bf16[32,32,3,3,3]{1,0,4,3,2:T(8,128)(2,1)}, u32[]{:S(2)}) copy-start(bf16[32,32,3,3,3]{1,0,4,3,2:T(8,128)(2,1)} %param.9) | copy-start | bytes 165892
  23.4 0.9 %copy-start.2 = (bf16[32,32,3,3,3]{1,0,4,3,2:T(8,128)(2,1)S(1)}, bf16[32,32,3,3,3]{1,0,4,3,2:T(8,128)(2,1)}, u32[]{:S(2)}) copy-start(bf16[32,32,3,3,3]{1,0,4,3,2:T(8,128)(2,1)} %param.10) | copy-start | bytes 165892
  29.7 0.6 %copy-start.3 = (bf16[8,16,128]{2,1,0:T(8,128)(2,1)}, bf16[8,16,128]{2,1,0:T(8,128)(2,1)S(1)}, u32[]{:S(2)}) copy-start(bf16[8,16,128]{2,1,0:T(8,128)(2,1)S(1)} %filter_columns.1.parts) | copy-start | bytes 98308
  40.2 1.4 %copy-start.4 = (f32[2,256]{1,0:T(2,128)S(1)}, f32[2,256]{1,0:T(2,128)}, u32[]{:S(2)}) copy-start(f32[2,256]{1,0:T(2,128)} %get-tuple-element.13) | copy-start | bytes 6148

commit v2 on v1

v2 whole, which is shorter than its diff:
```python
import jax
import jax.numpy as jnp
from jax import lax
from jax.experimental import pallas as pl
from jax.experimental.pallas import tpu as pltpu
from jax.sharding import PartitionSpec as P

N = 16
LANES = 128
DISP = 256
CH_ROWS = 40
WIDE_ROWS = 48
COLS0, COLS1, COLS2, COLS3 = 22, 20, 18, 16
F = 32
MASKED = -1e30
MESH = pl.DeviceIdType.MESH
NT = (((1,), (1,)), ((), ()))


def first_block(i):
    return lax.div(i + 7, 8) - 1


def places(block):
    for low, high, first in ((0, 0, -1), (1, 8, 0), (9, 15, 1)):
        slot = block - first
        if 0 <= slot < 4:
            yield slot, max(low, 7) if slot == 3 and high == 8 else low, high


def dot(a, b, dims=(((1,), (0,)), ((), ()))):
    return lax.dot_general(a, b, dims, preferred_element_type=jnp.float32)


def iota(shape, dim):
    return lax.broadcasted_iota(jnp.int32, shape, dim)


def one_hot(mask):
    return jnp.where(mask, 1.0, 0.0).astype(jnp.bfloat16)


def spread_first(weights, out):
    rows, lane = iota((CH_ROWS, LANES), 0), iota((CH_ROWS, LANES), 1)
    r = lane % 16
    flat = weights[...].reshape(27 * F, CH_ROWS)
    parts = [
        dot(flat, one_hot((rows == lane // 16 * 5 + r // 2) & (r < 10) & (r % 2 == h))) for h in range(2)
    ]
    parts = [part.reshape(3, 3, 3, F, LANES) for part in parts]
    for a in range(3):
        for to in range(2):
            for ho in range(2):
                row = ((a * 2 + to) * 2 + ho) * F
                for ti in range(4):
                    e = ti - to
                    if 0 <= e < 3:
                        block = parts[0][a, 1 - ho, e] + parts[1][a, 2 - ho, e]
                    else:
                        block = jnp.zeros((F, LANES), jnp.float32)
                    out[row : row + F, ti * LANES : (ti + 1) * LANES] = block.astype(jnp.bfloat16)


def spread_later(weights, out):
    rows, lane = iota((F, LANES), 0), iota((F, LANES), 1)
    flat = weights[...].reshape(27 * F, F)
    parts = [dot(flat, one_hot(rows == lane - k * F)).reshape(3, 3, 3, F, LANES) for k in range(4)]
    for a in range(3):
        for to in range(2):
            for ho in range(2):
                row = ((a * 2 + to) * 2 + ho) * F
                for pair in range(2):
                    block = jnp.zeros((F, LANES), jnp.float32)
                    for k in range(4):
                        e, h = pair * 2 + k // 2 - to, k % 2
                        if 0 <= e < 3:
                            block = block + parts[k][a, 1 + h - ho, e]
                    out[row : row + F, pair * LANES : (pair + 1) * LANES] = block.astype(jnp.bfloat16)


def filter_pair(kernel, x):
    taps = dot(kernel, x)
    rows = 2 * 2 * F
    lane = iota((rows, DISP), 1)
    before = jnp.where(lane == DISP - 1, 0.0, pltpu.roll(taps[:rows], DISP - 1, 1))
    after = jnp.where(lane == 0, 0.0, pltpu.roll(taps[2 * rows :], 1, 1))
    return jnp.maximum(taps[rows : 2 * rows] + before + after, 0.0)


def stereo_kernel(
    left_feat, right_feat, w1_hbm, w2_hbm, w3_hbm, head, warped, disparity_out,
    own, wide, near, parts, held, w1, w2, w3, k1, k2, k3, right, x0, x1, x2, scores,
    weight_sem, send_sem, recv_sem, result_send, result_recv,
):
    i, j = lax.axis_index("disp"), lax.axis_index("col")
    weights = ((w1_hbm, w1), (w2_hbm, w2), (w3_hbm, w3))
    for n, (src, dst) in enumerate(weights):
        pltpu.make_async_copy(src, dst, weight_sem.at[n]).start()
    for n, feat in enumerate((right_feat, left_feat)):
        flat = feat[...].astype(jnp.float32).reshape(CH_ROWS, 256).astype(jnp.bfloat16)
        for half in range(2):
            own[half, n * CH_ROWS : (n + 1) * CH_ROWS] = flat[:, half * LANES : (half + 1) * LANES]

    base = first_block(i)

    def slot_filled(q):
        block = 2 * (j - 1) + base + q
        filled = (block >= 0) & (block < 2 * N)
        if q == 3:
            filled = filled & ((lax.rem(i, 8) == 0) | (lax.rem(i, 8) == 7))
        return filled

    slots = [wide.at[0], wide.at[1], near.at[0], near.at[1]]
    for q in range(4):

        @pl.when(jnp.logical_not(slot_filled(q)))
        def _(q=q):
            slots[q][...] = jnp.zeros(slots[q].shape, jnp.bfloat16)

    barrier = pltpu.get_barrier_semaphore()

    def greet(di, dj):
        pl.semaphore_signal(barrier, inc=1, device_id=(di, dj), device_id_type=MESH)

    def greet_strip(dj):
        @pl.loop(0, N)
        def _(step):
            greet(lax.rem(i + step, N), dj)

    @pl.loop(1, N)
    def _(step):
        greet(lax.rem(i + step, N), j)

    pl.when(j >= 1)(lambda: greet_strip(j - 1))
    pl.when((i == 0) & (j >= 2))(lambda: greet_strip(j - 2))
    pl.when((i == N - 1) & (j <= N - 2))(lambda: greet_strip(j + 1))
    targets = N - 1 + N * (j <= N - 2) + (j <= N - 3) + (j >= 1)
    pl.semaphore_wait(barrier, targets)

    def copy(go, src, dst, slot, di, dj, sem):
        rdma = pltpu.make_async_remote_copy(
            src_ref=src,
            dst_ref=dst,
            send_sem=send_sem.at[sem],
            recv_sem=recv_sem.at[slot, lax.div(i, 2)],
            device_id=(di, dj),
            device_id_type=MESH,
        )
        rdma.start() if go else rdma.wait_send()

    def landing(half, slot):
        if slot < 2:
            return own.at[half, pl.ds(0, WIDE_ROWS)], wide.at[slot, i]
        return own.at[half], near.at[slot - 2, i]

    def push(go, di, dj, half, block, sem):
        for slot, low, high in places(block):

            @pl.when((di >= low) & (di <= high))
            def _(slot=slot):
                copy(go, *landing(half, slot), slot, di, dj, sem)

    def exchange(go):
        @pl.loop(0, N)
        def _(step):
            di = lax.rem(i + step, N)

            @pl.when(step > 0)
            def _():
                for half in range(2):
                    push(go, di, j, half, 2 + half, half * N + step)

            @pl.when(j <= N - 2)
            def _():
                for half in range(2):
                    push(go, di, j + 1, half, half, (2 + half) * N + step)

            @pl.when((di == 0) & (j <= N - 3))
            def _():
                copy(go, *landing(1, 0), 0, di, j + 2, 0)

            @pl.when((di == N - 1) & (j >= 1))
            def _():
                copy(go, *landing(0, 3), 3, di, j - 1, N)

    exchange(True)

    for half in range(2):
        for slot, low, high in places(2 + half):

            @pl.when((i >= low) & (i <= high))
            def _(half=half, slot=slot):
                pltpu.make_async_copy(*landing(half, slot), recv_sem.at[slot, lax.div(i, 2)]).start()

    for n, (src, dst) in enumerate(weights):
        pltpu.make_async_copy(src, dst, weight_sem.at[n]).wait()
    spread_first(w1, k1)
    spread_later(w2, k2)
    spread_later(w3, k3)

    start = 16 * i - 2 - LANES * base
    lane = iota((80, LANES), 1)
    r, lane80 = iota((16, 80), 0), iota((16, 80), 1)
    group_mask = jnp.where((lane80 // 16 == r // 2) & (lane80 % 2 == r % 2), 0.125, 0.0)
    pick = one_hot(iota((32, 2 * LANES), 1) == start - 1 + iota((32, 2 * LANES), 0))

    @pl.loop(0, 8)
    def _(n):
        s = lax.rem(lax.div(i, 2) + 8 - n, 8)
        pair = pl.ds(2 * s, 2)
        for q in range(4):

            @pl.when(slot_filled(q))
            def _(q=q):
                landed = slots[q].at[pair]
                pltpu.make_async_copy(landed, landed, recv_sem.at[q, s]).wait()

        blocks = [ref[q, pair].astype(jnp.float32) for ref in (wide, near) for q in range(2)]
        turned = [
            pltpu.roll(block[:, :CH_ROWS].reshape(80, LANES), LANES - start, 1) for block in blocks
        ]
        moved = [jnp.where(lane < LANES - start, turned[m], turned[m + 1]) for m in range(3)]
        moved = jnp.concatenate(moved, axis=1).astype(jnp.bfloat16)
        right[s] = moved
        left = [block[:, CH_ROWS:].reshape(80, LANES).astype(jnp.bfloat16) for block in blocks[2:]]
        picked = dot(pick[:, :LANES], left[0], NT) + dot(pick[:, LANES:], left[1], NT)
        spread = picked[:COLS0].reshape(COLS0, 1, 80) * group_mask[None]
        spread = spread.reshape(COLS0 * 16, 80).astype(jnp.bfloat16)
        products = dot(spread, moved)
        for k in range(COLS0):
            strip = products[k * 16 : (k + 1) * 16]
            if k:
                strip = pltpu.roll(strip, 3 * LANES - k, 1)
            place = pl.ds(pl.multiple_of(k * LANES + s * 16, 16), 16)
            x0[place] = strip[:, :DISP].astype(jnp.bfloat16)

    exchange(False)

    leftmost, rightmost = (i == 0) & (j == 0), (i == N - 1) & (j == N - 1)
    to = iota((LANES, DISP), 0) // 64
    for p in range(COLS1 // 2):
        y = filter_pair(k1[...], x0[p * 256 : p * 256 + 512])
        if p == 0:
            y = jnp.where(leftmost, 0.0, y)
        if p == COLS1 // 2 - 1:
            y = jnp.where(rightmost, 0.0, y)
        x1[p * LANES : (p + 1) * LANES] = y.astype(jnp.bfloat16)
    for p in range(COLS2 // 2):
        y = filter_pair(k2[...], x1[p * LANES : p * LANES + 256])
        if p == 0:
            y = jnp.where(leftmost & (to == 0), 0.0, y)
        if p == COLS2 // 2 - 1:
            y = jnp.where(rightmost & (to == 1), 0.0, y)
        x2[p * LANES : (p + 1) * LANES] = y.astype(jnp.bfloat16)
    for p in range(COLS3 // 2):
        y = filter_pair(k3[...], x2[p * LANES : p * LANES + 256])
        y = jnp.sum((y * head[...]).reshape(4, F, DISP), axis=1)
        for t in range(2):
            for h in range(2):
                row = h * 16 + 2 * p + t
                scores[row : row + 1] = y[2 * t + h : 2 * t + h + 1]

    disp = DISP - 1 - iota((32, DISP), 1)
    column = (N * j + i) * 16 + iota((32, DISP), 0) % 16
    valid = column >= disp
    score = jnp.where(valid, scores[...], MASKED)
    top = jnp.max(score, axis=1, keepdims=True)
    weighting = jnp.where(valid, jnp.exp(score - top), 0.0)
    denominator = jnp.sum(weighting, axis=1, keepdims=True)
    disparity = jnp.sum(weighting * disp.astype(jnp.float32), axis=1, keepdims=True) / denominator / DISP
    padded = jnp.concatenate([weighting, jnp.zeros((32, LANES), jnp.float32)], axis=1)
    band = jnp.concatenate(
        [pltpu.roll(padded[h * 16 : h * 16 + 16], 3, 1, stride=1, stride_axis=0) for h in range(2)], axis=0
    )
    high = band.astype(jnp.bfloat16)
    low = (band - high.astype(jnp.float32)).astype(jnp.bfloat16)
    band = jnp.concatenate([high, low], axis=0)
    out_lane = iota((16, LANES), 1)
    disp_high = disparity.astype(jnp.bfloat16).astype(jnp.float32)
    disp_low = disparity - disp_high
    tail = jnp.zeros((16, LANES), jnp.float32)
    for n, column_of in enumerate((disp_high[:16], disp_high[16:], disp_low[:16], disp_low[16:])):
        tail = jnp.where(out_lane == 80 + n, column_of, tail)
    even = iota((16, 80), 1) % 2 == 0

    def push_result(di, s, go):
        rdma = pltpu.make_async_remote_copy(
            src_ref=parts.at[s],
            dst_ref=held.at[i],
            send_sem=result_send.at[di],
            recv_sem=result_recv,
            device_id=(di, j),
            device_id_type=MESH,
        )
        rdma.start() if go else rdma.wait_send()

    def each_result(s, go):
        for core in range(2):
            di = 2 * s + core
            pl.when(di != i)(lambda di=di: push_result(di, s, go))

    @pl.loop(0, 8)
    def _(n):
        s = lax.rem(lax.div(i, 2) + 1 + n, 8)
        summed = dot(band, right[s], NT)
        mean = (summed[:32] + summed[32:]) / denominator
        picked = jnp.where(even, mean[:16], mean[16:])
        picked = jnp.concatenate([picked, jnp.zeros((16, LANES - 80), jnp.float32)], axis=1)
        parts[s] = jnp.where(out_lane < 80, picked, tail).astype(jnp.bfloat16)
        each_result(s, True)

    pltpu.make_async_copy(parts.at[lax.div(i, 2)], held.at[i], result_recv).start()
    pltpu.make_async_copy(held, held, result_recv).wait()
    pl.loop(0, 8)(lambda s: each_result(s, False))
    rows, lane = iota((48, LANES), 0), iota((48, LANES), 1)
    mine = lane == lax.rem(i, 2) * CH_ROWS + rows
    extra = (lane == 40 + rows) | (lane == 42 + rows)
    pick = one_hot((mine & (rows < CH_ROWS)) | (extra & (rows >= CH_ROWS) & (rows < CH_ROWS + 2)))
    result = dot(pick, held[...].reshape(256, LANES), NT)
    warped[...] = result[:CH_ROWS].reshape(20, 2, 256).astype(jnp.bfloat16)
    disparity_out[...] = result[CH_ROWS : CH_ROWS + 2]


def shards(left_feat, right_feat, conv1_w, conv2_w, conv3_w, head_w):
    w1, w2, w3 = (jnp.transpose(w, (2, 3, 4, 0, 1)) for w in (conv1_w, conv2_w, conv3_w))
    head = jnp.tile(head_w, 4).reshape(128, 1)
    vmem, anywhere = pl.BlockSpec(memory_space=pltpu.VMEM), pl.BlockSpec(memory_space=pl.ANY)
    bf16, dma = jnp.bfloat16, pltpu.SemaphoreType.DMA
    return pl.pallas_call(
        stereo_kernel,
        out_shape=(
            jax.ShapeDtypeStruct((20, 2, 256), bf16),
            jax.ShapeDtypeStruct((2, 256), jnp.float32),
        ),
        in_specs=[vmem, vmem, anywhere, anywhere, anywhere, vmem],
        out_specs=(vmem, vmem),
        scratch_shapes=[
            pltpu.VMEM((2, 2 * CH_ROWS, LANES), bf16),
            pltpu.VMEM((2, N, WIDE_ROWS, LANES), bf16),
            pltpu.VMEM((2, N, 2 * CH_ROWS, LANES), bf16),
            pltpu.VMEM((8, 16, LANES), bf16),
            pltpu.VMEM((N, 16, LANES), bf16),
            pltpu.VMEM(w1.shape, bf16),
            pltpu.VMEM(w2.shape, bf16),
            pltpu.VMEM(w3.shape, bf16),
            pltpu.VMEM((384, 512), bf16),
            pltpu.VMEM((384, 256), bf16),
            pltpu.VMEM((384, 256), bf16),
            pltpu.VMEM((8, 80, 384), bf16),
            pltpu.VMEM((COLS0 * 128, DISP), bf16),
            pltpu.VMEM((COLS1 * 64, DISP), bf16),
            pltpu.VMEM((COLS2 * 64, DISP), bf16),
            pltpu.VMEM((32, DISP), jnp.float32),
            dma((3,)),
            dma((4 * N,)),
            dma((4, 8)),
            dma((N,)),
            dma,
        ],
        compiler_params=pltpu.CompilerParams(
            collective_id=0, has_side_effects=True, vmem_limit_bytes=56 * 2**20
        ),
        name="stereo",
    )(left_feat, right_feat, w1, w2, w3, head)


def solution(mesh):
    return jax.shard_map(
        shards,
        mesh=mesh,
        in_specs=(P("disp", None, "col"), P("disp", None, "col"), P(), P(), P(), P()),
        out_specs=(P("disp", None, "col"), P(None, "col")),
        check_vma=False,
    )
```

time: 42.4 us -> 35.5 us (0.84)
  local copies, waits for them, and re-layouts: 6.7 us -> 3.3 us
  Pallas kernels: 34.7 us -> 31.4 us
    pallas_call x3 -> x1, Pallas kernels: 34.7 us -> 31.4 us  [shards(): pl.pallas_call(stereo_kernel, out_shape=(jax.ShapeDtypeStruct((20, 2, 256...]
    reshape x5 -> x0, local copies, waits for them, and re-layouts: 2.9 us -> none  [the longest x1 1.35 us: shards(): return (warped.reshape(20, 2, 256), disparity)]
    unnamed x13 -> x6, local copies, waits for them, and re-layouts: 3.69 us -> 2.58 us
    another operation x2, local copies, waits for them, and re-layouts: 0.11 us -> 0.72 us  [shards(): head = jnp.tile(head_w, 4).reshape(128, 1)]
where the time goes in v2:
time: 35.5 us; the launch traced here: 35.3 us
  Pallas kernels  31.4 us (88%)
  local copies, waits for them, and re-layouts  3.3 us (9%)
  between operations  0.66 us (2%)
    pallas_call x1, Pallas kernels, shards(): pl.pallas_call(stereo_kernel, out_shape=(jax.ShapeDtypeStruct((20, 2, 256...  31.4 us
    unnamed x6, local copies, waits for them, and re-layouts  2.58 us
    another operation x2, local copies, waits for them, and re-layouts, shards(): head = jnp.tile(head_w, 4).reshape(128, 1)  0.72 us

profile of v2, /device:TPU:129, one launch (start us, length us, event | category | flops | bytes accessed | tf_op | source)
XLA Modules:
  0.0 35.3 jit_solution(2149521327597979596)
XLA Ops:
  0.6 0.0 copy-start.1
  0.6 0.6 %copy-done.1 = f32[32]{0:T(128)S(1)} copy-done((f32[32]{0:T(128)S(1)}, f32[32]{0:T(128)}, u32[]{:S(2)}) %copy-start.1) | copy-done | bytes 152
  1.3 0.7 %reshape_tile.4.head = f32[128,1]{1,0:T(8,128)} reshape(f32[4,32]{1,0:T(4,128)S(1)} %tile.2) | data formatting | bytes 1024 | tf_op jit(solution)/shard_map/reshape;tile | solution.py:326
  2.0 31.4 %stereo.1 = (bf16[20,2,256]{2,1,0:T(2,128)(2,1)}, f32[2,256]{1,0:T(2,128)}) custom-call(bf16[20,2,256]{2,1,0:T(2,128)(2,1)} %left_feat.1, bf16[20,2,256]{2,1,0:T(2,128)(2,1)} %right_feat.1, bf16[3,3,3,32,40]{4,3,2,1,0:T(8,128)(2,1)} %bitcast.3, bf16[3,3,3,32,32]{4,3,2,1,0:T(8,128)(2,1)} %bitcast.4, bf16[3,3,3,32,32]{4,3,2,1,0:T(8,128)(2,1)} %bitcast.5, ...), custom_call_target="tpu_custom_call" | custom-call | tf_op jit(solution)/shard_map/stereo/pallas_call | solution.py:329
  33.4 0.0 copy-start
  33.4 1.3 %copy.11 = bf16[20,2,256]{2,1,0:T(2,128)(2,1)} copy(bf16[20,2,256]{2,1,0:T(2,128)(2,1)} %get-tuple-element.4) | data formatting | bytes 40960
  34.7 0.0 copy-done
  34.8 0.6 %copy.12 = f32[2,256]{1,0:T(2,128)} copy(f32[2,256]{1,0:T(2,128)S(1)} %copy-done) | data formatting | bytes 4096
  (1 shorter events, 0.0 us)
Async XLA Ops:
  0.6 0.7 %copy-start.1 = (f32[32]{0:T(128)S(1)}, f32[32]{0:T(128)}, u32[]{:S(2)}) copy-start(f32[32]{0:T(128)} %param.11) | copy-start | bytes 388
  33.4 1.4 %copy-start = (f32[2,256]{1,0:T(2,128)S(1)}, f32[2,256]{1,0:T(2,128)}, u32[]{:S(2)}) copy-start(f32[2,256]{1,0:T(2,128)} %get-tuple-element.5) | copy-start | bytes 6148

commit v3 on v2

--- a/solution.py
+++ b/solution.py
@@ -9,7 +9,9 @@
 LANES = 128
 DISP = 256
 CH_ROWS = 40
-WIDE_ROWS = 48
+SLOT_ROWS = (48, 48, 80, 80)
+SLOT_START = (0, 48, 96, 176)
+BASE_SHIFT = 14
 COLS0, COLS1, COLS2, COLS3 = 22, 20, 18, 16
 F = 32
 MASKED = -1e30
@@ -17,15 +19,15 @@
 NT = (((1,), (1,)), ((), ()))
 
 
-def first_block(i):
-    return lax.div(i + 7, 8) - 1
+def first_block(chip):
+    return lax.div(chip + 3, 4) - 1
 
 
 def places(block):
-    for low, high, first in ((0, 0, -1), (1, 8, 0), (9, 15, 1)):
+    for low, high, first in ((0, 0, -1), (1, 4, 0), (5, 7, 1)):
         slot = block - first
         if 0 <= slot < 4:
-            yield slot, max(low, 7) if slot == 3 and high == 8 else low, high
+            yield slot, max(low, 3) if slot == 3 and high == 4 else low, high
 
 
 def dot(a, b, dims=(((1,), (0,)), ((), ()))):
@@ -89,10 +91,12 @@
 
 def stereo_kernel(
     left_feat, right_feat, w1_hbm, w2_hbm, w3_hbm, head, warped, disparity_out,
-    own, wide, near, parts, held, w1, w2, w3, k1, k2, k3, right, x0, x1, x2, scores,
-    weight_sem, send_sem, recv_sem, result_send, result_recv,
+    own, land, parts, held, w1, w2, w3, k1, k2, k3, right, x0, x1, x2, scores,
+    weight_sem, send_sem, recv_sem, pass_send, pass_recv, result_send, result_recv,
 ):
     i, j = lax.axis_index("disp"), lax.axis_index("col")
+    chip, core = lax.div(i, 2), lax.rem(i, 2)
+    base = first_block(chip)
     weights = ((w1_hbm, w1), (w2_hbm, w2), (w3_hbm, w3))
     for n, (src, dst) in enumerate(weights):
         pltpu.make_async_copy(src, dst, weight_sem.at[n]).start()
@@ -101,21 +105,22 @@
         for half in range(2):
             own[half, n * CH_ROWS : (n + 1) * CH_ROWS] = flat[:, half * LANES : (half + 1) * LANES]
 
-    base = first_block(i)
-
-    def slot_filled(q):
-        block = 2 * (j - 1) + base + q
+    def slot_filled(slot):
+        block = 2 * (j - 1) + base + slot
         filled = (block >= 0) & (block < 2 * N)
-        if q == 3:
-            filled = filled & ((lax.rem(i, 8) == 0) | (lax.rem(i, 8) == 7))
+        if slot == 3:
+            filled = filled & ((lax.rem(chip, 4) == 0) | (lax.rem(chip, 4) == 3))
         return filled
 
-    slots = [wide.at[0], wide.at[1], near.at[0], near.at[1]]
-    for q in range(4):
-
-        @pl.when(jnp.logical_not(slot_filled(q)))
-        def _(q=q):
-            slots[q][...] = jnp.zeros(slots[q].shape, jnp.bfloat16)
+    def slot_rows(slot):
+        return pl.ds(SLOT_START[slot], SLOT_ROWS[slot])
+
+    for slot in range(4):
+
+        @pl.when(jnp.logical_not(slot_filled(slot)))
+        def _(slot=slot):
+            for n in range(8):
+                land[2 * n + core, slot_rows(slot)] = jnp.zeros((SLOT_ROWS[slot], LANES), jnp.bfloat16)
 
     barrier = pltpu.get_barrier_semaphore()
 
@@ -123,74 +128,73 @@
         pl.semaphore_signal(barrier, inc=1, device_id=(di, dj), device_id_type=MESH)
 
     def greet_strip(dj):
-        @pl.loop(0, N)
+        @pl.loop(0, 8)
         def _(step):
-            greet(lax.rem(i + step, N), dj)
+            greet(2 * lax.rem(chip + step, 8) + core, dj)
 
     @pl.loop(1, N)
     def _(step):
         greet(lax.rem(i + step, N), j)
 
     pl.when(j >= 1)(lambda: greet_strip(j - 1))
-    pl.when((i == 0) & (j >= 2))(lambda: greet_strip(j - 2))
-    pl.when((i == N - 1) & (j <= N - 2))(lambda: greet_strip(j + 1))
-    targets = N - 1 + N * (j <= N - 2) + (j <= N - 3) + (j >= 1)
+    pl.when((chip == 0) & (j >= 2))(lambda: greet_strip(j - 2))
+    pl.when((chip == 7) & (j <= N - 2))(lambda: greet_strip(j + 1))
+    targets = N - 1 + 8 * (j <= N - 2) + (j <= N - 3) + (j >= 1)
     pl.semaphore_wait(barrier, targets)
 
-    def copy(go, src, dst, slot, di, dj, sem):
+    def landing(half, slot):
+        return own.at[half, pl.ds(0, SLOT_ROWS[slot])], land.at[i, slot_rows(slot)]
+
+    def copy(go, half, slot, to_chip, dj, sem):
+        src, dst = landing(half, slot)
         rdma = pltpu.make_async_remote_copy(
             src_ref=src,
             dst_ref=dst,
             send_sem=send_sem.at[sem],
-            recv_sem=recv_sem.at[slot, lax.div(i, 2)],
-            device_id=(di, dj),
+            recv_sem=recv_sem.at[slot, chip],
+            device_id=(2 * to_chip + core, dj),
             device_id_type=MESH,
         )
         rdma.start() if go else rdma.wait_send()
 
-    def landing(half, slot):
-        if slot < 2:
-            return own.at[half, pl.ds(0, WIDE_ROWS)], wide.at[slot, i]
-        return own.at[half], near.at[slot - 2, i]
-
-    def push(go, di, dj, half, block, sem):
+    def push(go, to_chip, dj, half, block, sem):
         for slot, low, high in places(block):
 
-            @pl.when((di >= low) & (di <= high))
+            @pl.when((to_chip >= low) & (to_chip <= high))
             def _(slot=slot):
-                copy(go, *landing(half, slot), slot, di, dj, sem)
+                copy(go, half, slot, to_chip, dj, sem)
 
     def exchange(go):
-        @pl.loop(0, N)
+        @pl.loop(0, 8)
         def _(step):
-            di = lax.rem(i + step, N)
+            to_chip = lax.rem(chip + step, 8)
 
             @pl.when(step > 0)
             def _():
                 for half in range(2):
-                    push(go, di, j, half, 2 + half, half * N + step)
+                    push(go, to_chip, j, half, 2 + half, half * 8 + step)
 
             @pl.when(j <= N - 2)
             def _():
                 for half in range(2):
-                    push(go, di, j + 1, half, half, (2 + half) * N + step)
-
-            @pl.when((di == 0) & (j <= N - 3))
+                    push(go, to_chip, j + 1, half, half, (2 + half) * 8 + step)
+
+            @pl.when((to_chip == 0) & (j <= N - 3))
             def _():
-                copy(go, *landing(1, 0), 0, di, j + 2, 0)
-
-            @pl.when((di == N - 1) & (j >= 1))
+                copy(go, 1, 0, to_chip, j + 2, 0)
+
+            @pl.when((to_chip == 7) & (j >= 1))
             def _():
-                copy(go, *landing(0, 3), 3, di, j - 1, N)
+                copy(go, 0, 3, to_chip, j - 1, 8)
 
     exchange(True)
 
     for half in range(2):
         for slot, low, high in places(2 + half):
 
-            @pl.when((i >= low) & (i <= high))
+            @pl.when((chip >= low) & (chip <= high))
             def _(half=half, slot=slot):
-                pltpu.make_async_copy(*landing(half, slot), recv_sem.at[slot, lax.div(i, 2)]).start()
+                pltpu.make_async_copy(*landing(half, slot), recv_sem.at[slot, chip]).start()
 
     for n, (src, dst) in enumerate(weights):
         pltpu.make_async_copy(src, dst, weight_sem.at[n]).wait()
@@ -198,24 +202,45 @@
     spread_later(w2, k2)
     spread_later(w3, k3)
 
-    start = 16 * i - 2 - LANES * base
+    start = 16 * i - 2 - BASE_SHIFT - LANES * base
     lane = iota((80, LANES), 1)
     r, lane80 = iota((16, 80), 0), iota((16, 80), 1)
     group_mask = jnp.where((lane80 // 16 == r // 2) & (lane80 % 2 == r % 2), 0.125, 0.0)
-    pick = one_hot(iota((32, 2 * LANES), 1) == start - 1 + iota((32, 2 * LANES), 0))
+    pick = one_hot(iota((32, 2 * LANES), 1) == start + BASE_SHIFT - 1 + iota((32, 2 * LANES), 0))
+
+    def pass_on(s, go):
+        held_here = land.at[2 * s + core]
+        rdma = pltpu.make_async_remote_copy(
+            src_ref=held_here,
+            dst_ref=held_here,
+            send_sem=pass_send.at[s],
+            recv_sem=pass_recv.at[s],
+            device_id=(2 * chip + 1 - core, j),
+            device_id_type=MESH,
+        )
+        rdma.start() if go else rdma.wait_send()
+
+    def arrive(n):
+        s = lax.rem(chip + 8 - n, 8)
+        for slot in range(4):
+
+            @pl.when(slot_filled(slot))
+            def _(slot=slot):
+                landed = land.at[2 * s + core, slot_rows(slot)]
+                pltpu.make_async_copy(landed, landed, recv_sem.at[slot, s]).wait()
+
+        pass_on(s, True)
+
+    arrive(0)
 
     @pl.loop(0, 8)
     def _(n):
-        s = lax.rem(lax.div(i, 2) + 8 - n, 8)
+        pl.when(n < 7)(lambda: arrive(n + 1))
+        s = lax.rem(chip + 8 - n, 8)
         pair = pl.ds(2 * s, 2)
-        for q in range(4):
-
-            @pl.when(slot_filled(q))
-            def _(q=q):
-                landed = slots[q].at[pair]
-                pltpu.make_async_copy(landed, landed, recv_sem.at[q, s]).wait()
-
-        blocks = [ref[q, pair].astype(jnp.float32) for ref in (wide, near) for q in range(2)]
+        passed = land.at[2 * s + 1 - core]
+        pltpu.make_async_copy(passed, passed, pass_recv.at[s]).wait()
+        blocks = [land[pair, slot_rows(slot)].astype(jnp.float32) for slot in range(4)]
         turned = [
             pltpu.roll(block[:, :CH_ROWS].reshape(80, LANES), LANES - start, 1) for block in blocks
         ]
@@ -229,12 +254,14 @@
         products = dot(spread, moved)
         for k in range(COLS0):
             strip = products[k * 16 : (k + 1) * 16]
-            if k:
-                strip = pltpu.roll(strip, 3 * LANES - k, 1)
+            strip = pltpu.roll(strip, 3 * LANES - BASE_SHIFT - k, 1)
             place = pl.ds(pl.multiple_of(k * LANES + s * 16, 16), 16)
             x0[place] = strip[:, :DISP].astype(jnp.bfloat16)
 
     exchange(False)
+    pl.loop(0, 8)(lambda s: pass_on(s, False))
+    head_rows = jnp.where(iota((LANES, F), 0) % F == iota((LANES, F), 1), head[...], 0.0)
+    head_column = jnp.sum(head_rows, axis=1, keepdims=True)
 
     leftmost, rightmost = (i == 0) & (j == 0), (i == N - 1) & (j == N - 1)
     to = iota((LANES, DISP), 0) // 64
@@ -254,7 +281,7 @@
         x2[p * LANES : (p + 1) * LANES] = y.astype(jnp.bfloat16)
     for p in range(COLS3 // 2):
         y = filter_pair(k3[...], x2[p * LANES : p * LANES + 256])
-        y = jnp.sum((y * head[...]).reshape(4, F, DISP), axis=1)
+        y = jnp.sum((y * head_column).reshape(4, F, DISP), axis=1)
         for t in range(2):
             for h in range(2):
                 row = h * 16 + 2 * p + t
@@ -270,7 +297,7 @@
     disparity = jnp.sum(weighting * disp.astype(jnp.float32), axis=1, keepdims=True) / denominator / DISP
     padded = jnp.concatenate([weighting, jnp.zeros((32, LANES), jnp.float32)], axis=1)
     band = jnp.concatenate(
-        [pltpu.roll(padded[h * 16 : h * 16 + 16], 3, 1, stride=1, stride_axis=0) for h in range(2)], axis=0
+        [pltpu.roll(padded[h * 16 : h * 16 + 16], BASE_SHIFT + 3, 1, stride=1, stride_axis=0) for h in range(2)], axis=0
     )
     high = band.astype(jnp.bfloat16)
     low = (band - high.astype(jnp.float32)).astype(jnp.bfloat16)
@@ -301,7 +328,7 @@
 
     @pl.loop(0, 8)
     def _(n):
-        s = lax.rem(lax.div(i, 2) + 1 + n, 8)
+        s = lax.rem(chip + 1 + n, 8)
         summed = dot(band, right[s], NT)
         mean = (summed[:32] + summed[32:]) / denominator
         picked = jnp.where(even, mean[:16], mean[16:])
@@ -309,7 +336,7 @@
         parts[s] = jnp.where(out_lane < 80, picked, tail).astype(jnp.bfloat16)
         each_result(s, True)
 
-    pltpu.make_async_copy(parts.at[lax.div(i, 2)], held.at[i], result_recv).start()
+    pltpu.make_async_copy(parts.at[chip], held.at[i], result_recv).start()
     pltpu.make_async_copy(held, held, result_recv).wait()
     pl.loop(0, 8)(lambda s: each_result(s, False))
     rows, lane = iota((48, LANES), 0), iota((48, LANES), 1)
@@ -323,7 +350,7 @@
 
 def shards(left_feat, right_feat, conv1_w, conv2_w, conv3_w, head_w):
     w1, w2, w3 = (jnp.transpose(w, (2, 3, 4, 0, 1)) for w in (conv1_w, conv2_w, conv3_w))
-    head = jnp.tile(head_w, 4).reshape(128, 1)
+    head = head_w.reshape(1, F)
     vmem, anywhere = pl.BlockSpec(memory_space=pltpu.VMEM), pl.BlockSpec(memory_space=pl.ANY)
     bf16, dma = jnp.bfloat16, pltpu.SemaphoreType.DMA
     return pl.pallas_call(
@@ -336,8 +363,7 @@
         out_specs=(vmem, vmem),
         scratch_shapes=[
             pltpu.VMEM((2, 2 * CH_ROWS, LANES), bf16),
-            pltpu.VMEM((2, N, WIDE_ROWS, LANES), bf16),
-            pltpu.VMEM((2, N, 2 * CH_ROWS, LANES), bf16),
+            pltpu.VMEM((N, 256, LANES), bf16),
             pltpu.VMEM((8, 16, LANES), bf16),
             pltpu.VMEM((N, 16, LANES), bf16),
             pltpu.VMEM(w1.shape, bf16),
@@ -352,8 +378,10 @@
             pltpu.VMEM((COLS2 * 64, DISP), bf16),
             pltpu.VMEM((32, DISP), jnp.float32),
             dma((3,)),
-            dma((4 * N,)),
+            dma((4 * 8,)),
             dma((4, 8)),
+            dma((8,)),
+            dma((8,)),
             dma((N,)),
             dma,
         ],

time: 35.5 us -> 31.4 us (0.88)
  the two profiles are of different devices: /device:TPU:129 before, /device:TPU:1 now
where the time goes in v3:
time: 31.4 us; the launch traced here: 31.2 us
  Pallas kernels  28.6 us (91%)
  local copies, waits for them, and re-layouts  1.93 us (6%)
  between operations  0.65 us (2%)
    pallas_call x1, Pallas kernels, shards(): pl.pallas_call(stereo_kernel, out_shape=(jax.ShapeDtypeStruct((20, 2, 256...  28.6 us
    unnamed x4, local copies, waits for them, and re-layouts  1.93 us

profile of v3, /device:TPU:1, one launch (start us, length us, event | category | flops | bytes accessed | tf_op | source)
XLA Modules:
  0.0 31.2 jit_solution(2990930406561201677)
XLA Ops:
  0.6 28.6 %stereo.1 = (bf16[20,2,256]{2,1,0:T(2,128)(2,1)}, f32[2,256]{1,0:T(2,128)}) custom-call(bf16[20,2,256]{2,1,0:T(2,128)(2,1)} %left_feat.1, bf16[20,2,256]{2,1,0:T(2,128)(2,1)} %right_feat.1, bf16[3,3,3,32,40]{4,3,2,1,0:T(8,128)(2,1)} %bitcast.4, bf16[3,3,3,32,32]{4,3,2,1,0:T(8,128)(2,1)} %bitcast.5, bf16[3,3,3,32,32]{4,3,2,1,0:T(8,128)(2,1)} %bitcast.6, ...), custom_call_target="tpu_custom_call" | custom-call | tf_op jit(solution)/shard_map/stereo/pallas_call | solution.py:356
  29.3 0.0 copy-start
  29.3 1.3 %copy.10 = bf16[20,2,256]{2,1,0:T(2,128)(2,1)} copy(bf16[20,2,256]{2,1,0:T(2,128)(2,1)} %get-tuple-element.4) | data formatting | bytes 40960
  30.6 0.0 copy-done
  30.6 0.6 %copy.11 = f32[2,256]{1,0:T(2,128)} copy(f32[2,256]{1,0:T(2,128)S(1)} %copy-done) | data formatting | bytes 4096
Async XLA Ops:
  29.3 1.4 %copy-start = (f32[2,256]{1,0:T(2,128)S(1)}, f32[2,256]{1,0:T(2,128)}, u32[]{:S(2)}) copy-start(f32[2,256]{1,0:T(2,128)} %get-tuple-element.5) | copy-start | bytes 6148

commit v4 on v3

--- a/solution.py
+++ b/solution.py
@@ -90,21 +90,13 @@
 
 
 def stereo_kernel(
-    left_feat, right_feat, w1_hbm, w2_hbm, w3_hbm, head, warped, disparity_out,
-    own, land, parts, held, w1, w2, w3, k1, k2, k3, right, x0, x1, x2, scores,
-    weight_sem, send_sem, recv_sem, pass_send, pass_recv, result_send, result_recv,
+    left_feat, right_feat, w1_hbm, w2_hbm, w3_hbm, head, held,
+    right_own, left_own, own, land, parts, w1, w2, w3, k1, k2, k3, right, x0, x1, x2, scores,
+    feature_sem, weight_sem, send_sem, recv_sem, pass_send, pass_recv, result_send, result_recv,
 ):
     i, j = lax.axis_index("disp"), lax.axis_index("col")
     chip, core = lax.div(i, 2), lax.rem(i, 2)
     base = first_block(chip)
-    weights = ((w1_hbm, w1), (w2_hbm, w2), (w3_hbm, w3))
-    for n, (src, dst) in enumerate(weights):
-        pltpu.make_async_copy(src, dst, weight_sem.at[n]).start()
-    for n, feat in enumerate((right_feat, left_feat)):
-        flat = feat[...].astype(jnp.float32).reshape(CH_ROWS, 256).astype(jnp.bfloat16)
-        for half in range(2):
-            own[half, n * CH_ROWS : (n + 1) * CH_ROWS] = flat[:, half * LANES : (half + 1) * LANES]
-
     def slot_filled(slot):
         block = 2 * (j - 1) + base + slot
         filled = (block >= 0) & (block < 2 * N)
@@ -115,6 +107,29 @@
     def slot_rows(slot):
         return pl.ds(SLOT_START[slot], SLOT_ROWS[slot])
 
+    barrier = pltpu.get_barrier_semaphore()
+
+    def greet(di, dj):
+        pl.semaphore_signal(barrier, inc=1, device_id=(di, dj), device_id_type=MESH)
+
+    def greet_strip(dj):
+        @pl.loop(0, 8)
+        def _(step):
+            greet(2 * lax.rem(chip + step, 8) + core, dj)
+
+    @pl.loop(1, N)
+    def _(step):
+        greet(lax.rem(i + step, N), j)
+
+    pl.when(j >= 1)(lambda: greet_strip(j - 1))
+    pl.when((chip == 0) & (j >= 2))(lambda: greet_strip(j - 2))
+    pl.when((chip == 7) & (j <= N - 2))(lambda: greet_strip(j + 1))
+    features = ((right_feat, right_own), (left_feat, left_own))
+    for n, (src, dst) in enumerate(features):
+        pltpu.make_async_copy(src, dst, feature_sem.at[n]).start()
+    weights = ((w1_hbm, w1), (w2_hbm, w2), (w3_hbm, w3))
+    for n, (src, dst) in enumerate(weights):
+        pltpu.make_async_copy(src, dst, weight_sem.at[n]).start()
     for slot in range(4):
 
         @pl.when(jnp.logical_not(slot_filled(slot)))
@@ -122,23 +137,14 @@
             for n in range(8):
                 land[2 * n + core, slot_rows(slot)] = jnp.zeros((SLOT_ROWS[slot], LANES), jnp.bfloat16)
 
-    barrier = pltpu.get_barrier_semaphore()
-
-    def greet(di, dj):
-        pl.semaphore_signal(barrier, inc=1, device_id=(di, dj), device_id_type=MESH)
-
-    def greet_strip(dj):
-        @pl.loop(0, 8)
-        def _(step):
-            greet(2 * lax.rem(chip + step, 8) + core, dj)
-
-    @pl.loop(1, N)
-    def _(step):
-        greet(lax.rem(i + step, N), j)
-
-    pl.when(j >= 1)(lambda: greet_strip(j - 1))
-    pl.when((chip == 0) & (j >= 2))(lambda: greet_strip(j - 2))
-    pl.when((chip == 7) & (j <= N - 2))(lambda: greet_strip(j + 1))
+    head_rows = jnp.where(iota((LANES, F), 0) % F == iota((LANES, F), 1), head[...], 0.0)
+    head_column = jnp.sum(head_rows, axis=1, keepdims=True)
+    for n, (src, dst) in enumerate(features):
+        pltpu.make_async_copy(src, dst, feature_sem.at[n]).wait()
+        flat = dst[...].astype(jnp.float32).reshape(CH_ROWS, 256).astype(jnp.bfloat16)
+        for half in range(2):
+            own[half, n * CH_ROWS : (n + 1) * CH_ROWS] = flat[:, half * LANES : (half + 1) * LANES]
+
     targets = N - 1 + 8 * (j <= N - 2) + (j <= N - 3) + (j >= 1)
     pl.semaphore_wait(barrier, targets)
 
@@ -231,11 +237,12 @@
 
         pass_on(s, True)
 
-    arrive(0)
+    for n in range(2):
+        arrive(n)
 
     @pl.loop(0, 8)
     def _(n):
-        pl.when(n < 7)(lambda: arrive(n + 1))
+        pl.when(n < 6)(lambda: arrive(n + 2))
         s = lax.rem(chip + 8 - n, 8)
         pair = pl.ds(2 * s, 2)
         passed = land.at[2 * s + 1 - core]
@@ -257,11 +264,6 @@
             strip = pltpu.roll(strip, 3 * LANES - BASE_SHIFT - k, 1)
             place = pl.ds(pl.multiple_of(k * LANES + s * 16, 16), 16)
             x0[place] = strip[:, :DISP].astype(jnp.bfloat16)
-
-    exchange(False)
-    pl.loop(0, 8)(lambda s: pass_on(s, False))
-    head_rows = jnp.where(iota((LANES, F), 0) % F == iota((LANES, F), 1), head[...], 0.0)
-    head_column = jnp.sum(head_rows, axis=1, keepdims=True)
 
     leftmost, rightmost = (i == 0) & (j == 0), (i == N - 1) & (j == N - 1)
     to = iota((LANES, DISP), 0) // 64
@@ -326,19 +328,23 @@
             di = 2 * s + core
             pl.when(di != i)(lambda di=di: push_result(di, s, go))
 
-    @pl.loop(0, 8)
-    def _(n):
-        s = lax.rem(chip + 1 + n, 8)
+    for s in range(8):
         summed = dot(band, right[s], NT)
         mean = (summed[:32] + summed[32:]) / denominator
         picked = jnp.where(even, mean[:16], mean[16:])
         picked = jnp.concatenate([picked, jnp.zeros((16, LANES - 80), jnp.float32)], axis=1)
         parts[s] = jnp.where(out_lane < 80, picked, tail).astype(jnp.bfloat16)
-        each_result(s, True)
-
+
+    pl.loop(0, 8)(lambda n: each_result(lax.rem(chip + 4 + n, 8), True))
     pltpu.make_async_copy(parts.at[chip], held.at[i], result_recv).start()
+    exchange(False)
+    pl.loop(0, 8)(lambda s: pass_on(s, False))
+    pl.loop(0, 8)(lambda s: each_result(s, False))
     pltpu.make_async_copy(held, held, result_recv).wait()
-    pl.loop(0, 8)(lambda s: each_result(s, False))
+
+
+def finish_kernel(held, warped, disparity_out):
+    i = lax.axis_index("disp")
     rows, lane = iota((48, LANES), 0), iota((48, LANES), 1)
     mine = lane == lax.rem(i, 2) * CH_ROWS + rows
     extra = (lane == 40 + rows) | (lane == 42 + rows)
@@ -353,19 +359,17 @@
     head = head_w.reshape(1, F)
     vmem, anywhere = pl.BlockSpec(memory_space=pltpu.VMEM), pl.BlockSpec(memory_space=pl.ANY)
     bf16, dma = jnp.bfloat16, pltpu.SemaphoreType.DMA
-    return pl.pallas_call(
+    held = pl.pallas_call(
         stereo_kernel,
-        out_shape=(
-            jax.ShapeDtypeStruct((20, 2, 256), bf16),
-            jax.ShapeDtypeStruct((2, 256), jnp.float32),
-        ),
-        in_specs=[vmem, vmem, anywhere, anywhere, anywhere, vmem],
-        out_specs=(vmem, vmem),
+        out_shape=jax.ShapeDtypeStruct((N, 16, LANES), bf16),
+        in_specs=[anywhere] * 5 + [vmem],
+        out_specs=vmem,
         scratch_shapes=[
+            pltpu.VMEM((20, 2, 256), bf16),
+            pltpu.VMEM((20, 2, 256), bf16),
             pltpu.VMEM((2, 2 * CH_ROWS, LANES), bf16),
             pltpu.VMEM((N, 256, LANES), bf16),
             pltpu.VMEM((8, 16, LANES), bf16),
-            pltpu.VMEM((N, 16, LANES), bf16),
             pltpu.VMEM(w1.shape, bf16),
             pltpu.VMEM(w2.shape, bf16),
             pltpu.VMEM(w3.shape, bf16),
@@ -377,6 +381,7 @@
             pltpu.VMEM((COLS1 * 64, DISP), bf16),
             pltpu.VMEM((COLS2 * 64, DISP), bf16),
             pltpu.VMEM((32, DISP), jnp.float32),
+            dma((2,)),
             dma((3,)),
             dma((4 * 8,)),
             dma((4, 8)),
@@ -390,6 +395,16 @@
         ),
         name="stereo",
     )(left_feat, right_feat, w1, w2, w3, head)
+    return pl.pallas_call(
+        finish_kernel,
+        out_shape=(
+            jax.ShapeDtypeStruct((20, 2, 256), bf16),
+            jax.ShapeDtypeStruct((2, 256), jnp.float32),
+        ),
+        in_specs=[vmem],
+        out_specs=(vmem, vmem),
+        name="finish",
+    )(held)
 
 
 def solution(mesh):

time: 31.4 us -> 29.9 us (0.952)
  local copies, waits for them, and re-layouts: 1.93 us -> 0 us
  Pallas kernels: 28.6 us -> 29.1 us
    unnamed x4 -> x0, local copies, waits for them, and re-layouts: 1.93 us -> none
    pallas_call x1 -> x2, Pallas kernels: 28.6 us -> 29.1 us  [the longest x1 27.4 us: shards(): pl.pallas_call(stereo_kernel, out_shape=jax.ShapeDtypeStruct((N, 16, LANE...]
where the time goes in v4:
time: 29.9 us; the launch traced here: 29.7 us
  Pallas kernels  29.1 us (97%)
  between operations  0.64 us (2%)
    pallas_call x1, Pallas kernels, shards(): pl.pallas_call(stereo_kernel, out_shape=jax.ShapeDtypeStruct((N, 16, LANE...  27.4 us
    pallas_call x1, Pallas kernels, shards(): pl.pallas_call(finish_kernel, out_shape=(jax.ShapeDtypeStruct((20, 2, 256...  1.62 us

profile of v4, /device:TPU:1, one launch (start us, length us, event | category | flops | bytes accessed | tf_op | source)
XLA Modules:
  0.0 29.7 jit_solution(6419232842506676894)
XLA Ops:
  0.6 27.4 %stereo.1.held = bf16[16,16,128]{2,1,0:T(8,128)(2,1)} custom-call(bf16[20,2,256]{2,1,0:T(2,128)(2,1)} %left_feat.1, bf16[20,2,256]{2,1,0:T(2,128)(2,1)} %right_feat.1, bf16[3,3,3,32,40]{4,3,2,1,0:T(8,128)(2,1)} %bitcast.4, bf16[3,3,3,32,32]{4,3,2,1,0:T(8,128)(2,1)} %bitcast.5, bf16[3,3,3,32,32]{4,3,2,1,0:T(8,128)(2,1)} %bitcast.6, f32[1,32]{1,0:T(1,128)} %bitcast.7), custom_call_target="tpu_custom_call" | custom-call | tf_op jit(solution)/shard_map/stereo/pallas_call | solution.py:362
  28.1 1.6 %finish.1 = (bf16[20,2,256]{2,1,0:T(2,128)(2,1)}, f32[2,256]{1,0:T(2,128)}) custom-call(bf16[16,16,128]{2,1,0:T(8,128)(2,1)} %stereo.1.held), custom_call_target="tpu_custom_call" | custom-call | tf_op jit(solution)/shard_map/finish/pallas_call | solution.py:398

commit v5 on v4

--- a/solution.py
+++ b/solution.py
@@ -145,6 +145,12 @@
         for half in range(2):
             own[half, n * CH_ROWS : (n + 1) * CH_ROWS] = flat[:, half * LANES : (half + 1) * LANES]
 
+    for n, (src, dst) in enumerate(weights):
+        pltpu.make_async_copy(src, dst, weight_sem.at[n]).wait()
+    spread_first(w1, k1)
+    spread_later(w2, k2)
+    spread_later(w3, k3)
+
     targets = N - 1 + 8 * (j <= N - 2) + (j <= N - 3) + (j >= 1)
     pl.semaphore_wait(barrier, targets)
 
@@ -201,12 +207,6 @@
             @pl.when((chip >= low) & (chip <= high))
             def _(half=half, slot=slot):
                 pltpu.make_async_copy(*landing(half, slot), recv_sem.at[slot, chip]).start()
-
-    for n, (src, dst) in enumerate(weights):
-        pltpu.make_async_copy(src, dst, weight_sem.at[n]).wait()
-    spread_first(w1, k1)
-    spread_later(w2, k2)
-    spread_later(w3, k3)
 
     start = 16 * i - 2 - BASE_SHIFT - LANES * base
     lane = iota((80, LANES), 1)
@@ -335,7 +335,7 @@
         picked = jnp.concatenate([picked, jnp.zeros((16, LANES - 80), jnp.float32)], axis=1)
         parts[s] = jnp.where(out_lane < 80, picked, tail).astype(jnp.bfloat16)
 
-    pl.loop(0, 8)(lambda n: each_result(lax.rem(chip + 4 + n, 8), True))
+    pl.loop(0, 8)(lambda n: each_result(lax.rem(chip + 1 + n, 8), True))
     pltpu.make_async_copy(parts.at[chip], held.at[i], result_recv).start()
     exchange(False)
     pl.loop(0, 8)(lambda s: pass_on(s, False))

time: 29.9 us -> 29.7 us (level)
  no operation moved by 1% of the time
where the time goes in v5:
time: 29.7 us; the launch traced here: 29.5 us
  Pallas kernels  28.9 us (97%)
  between operations  0.64 us (2%)
    pallas_call x1, Pallas kernels, shards(): pl.pallas_call(stereo_kernel, out_shape=jax.ShapeDtypeStruct((N, 16, LANE...  27.2 us
    pallas_call x1, Pallas kernels, shards(): pl.pallas_call(finish_kernel, out_shape=(jax.ShapeDtypeStruct((20, 2, 256...  1.62 us

profile of v5, /device:TPU:1, one launch (start us, length us, event | category | flops | bytes accessed | tf_op | source)
XLA Modules:
  0.0 29.5 jit_solution(16292184104463611901)
XLA Ops:
  0.6 27.2 %stereo.1.held = bf16[16,16,128]{2,1,0:T(8,128)(2,1)} custom-call(bf16[20,2,256]{2,1,0:T(2,128)(2,1)} %left_feat.1, bf16[20,2,256]{2,1,0:T(2,128)(2,1)} %right_feat.1, bf16[3,3,3,32,40]{4,3,2,1,0:T(8,128)(2,1)} %bitcast.4, bf16[3,3,3,32,32]{4,3,2,1,0:T(8,128)(2,1)} %bitcast.5, bf16[3,3,3,32,32]{4,3,2,1,0:T(8,128)(2,1)} %bitcast.6, f32[1,32]{1,0:T(1,128)} %bitcast.7), custom_call_target="tpu_custom_call" | custom-call | tf_op jit(solution)/shard_map/stereo/pallas_call | solution.py:362
  27.9 1.6 %finish.1 = (bf16[20,2,256]{2,1,0:T(2,128)(2,1)}, f32[2,256]{1,0:T(2,128)}) custom-call(bf16[16,16,128]{2,1,0:T(8,128)(2,1)} %stereo.1.held), custom_call_target="tpu_custom_call" | custom-call | tf_op jit(solution)/shard_map/finish/pallas_call | solution.py:398

commit v6 on v5

--- a/solution.py
+++ b/solution.py
@@ -242,7 +242,6 @@
 
     @pl.loop(0, 8)
     def _(n):
-        pl.when(n < 6)(lambda: arrive(n + 2))
         s = lax.rem(chip + 8 - n, 8)
         pair = pl.ds(2 * s, 2)
         passed = land.at[2 * s + 1 - core]
@@ -264,6 +263,8 @@
             strip = pltpu.roll(strip, 3 * LANES - BASE_SHIFT - k, 1)
             place = pl.ds(pl.multiple_of(k * LANES + s * 16, 16), 16)
             x0[place] = strip[:, :DISP].astype(jnp.bfloat16)
+
+        pl.when(n < 6)(lambda: arrive(n + 2))
 
     leftmost, rightmost = (i == 0) & (j == 0), (i == N - 1) & (j == N - 1)
     to = iota((LANES, DISP), 0) // 64

time: 29.7 us -> 30.2 us (1.017)
  Pallas kernels: 28.9 us -> 29.4 us
    pallas_call x1, Pallas kernels: 27.2 us -> 27.8 us  [shards(): pl.pallas_call(stereo_kernel, out_shape=jax.ShapeDtypeStruct((N, 16, LANE...]
where the time goes in v6:
time: 30.2 us; the launch traced here: 30.1 us
  Pallas kernels  29.4 us (97%)
  between operations  0.64 us (2%)
    pallas_call x1, Pallas kernels, shards(): pl.pallas_call(stereo_kernel, out_shape=jax.ShapeDtypeStruct((N, 16, LANE...  27.8 us
    pallas_call x1, Pallas kernels, shards(): pl.pallas_call(finish_kernel, out_shape=(jax.ShapeDtypeStruct((20, 2, 256...  1.62 us

profile of v6, /device:TPU:1, one launch (start us, length us, event | category | flops | bytes accessed | tf_op | source)
XLA Modules:
  0.0 30.1 jit_solution(775505040167472666)
XLA Ops:
  0.6 27.8 %stereo.1.held = bf16[16,16,128]{2,1,0:T(8,128)(2,1)} custom-call(bf16[20,2,256]{2,1,0:T(2,128)(2,1)} %left_feat.1, bf16[20,2,256]{2,1,0:T(2,128)(2,1)} %right_feat.1, bf16[3,3,3,32,40]{4,3,2,1,0:T(8,128)(2,1)} %bitcast.4, bf16[3,3,3,32,32]{4,3,2,1,0:T(8,128)(2,1)} %bitcast.5, bf16[3,3,3,32,32]{4,3,2,1,0:T(8,128)(2,1)} %bitcast.6, f32[1,32]{1,0:T(1,128)} %bitcast.7), custom_call_target="tpu_custom_call" | custom-call | tf_op jit(solution)/shard_map/stereo/pallas_call | solution.py:363
  28.5 1.6 %finish.1 = (bf16[20,2,256]{2,1,0:T(2,128)(2,1)}, f32[2,256]{1,0:T(2,128)}) custom-call(bf16[16,16,128]{2,1,0:T(8,128)(2,1)} %stereo.1.held), custom_call_target="tpu_custom_call" | custom-call | tf_op jit(solution)/shard_map/finish/pallas_call | solution.py:399
